TPU v7x, 512 devices: a whole 4x4x16 slice. The times are simulated.
512 devices in a mesh: lat: 16 (over z_lo, y), row: 32 (over z_hi, x, core).
Axes of the slice: x: 4, y: 4, z: 16 (z_hi: 4, z_lo: 4; z = z_hi * 4 + z_lo), core: 2. Of those that a mesh axis runs over, the one named last changes fastest.
Arguments:
- g_wannier: bfloat16 [96, 300, 128, 256], P('lat', None, 'row'), may hold values from -0.8984375 to 0.8984375
- lattice: int32 [96, 3], P('lat'), may hold values from -6 to 6
- degeneracy: int32 [96], P('lat'), may hold values from 1 to 5
- qgrid: int32 [8, 3], replicated, may hold values from 0 to 39
- phonon_vectors: bfloat16 [8, 288, 600], P(None, 'lat'), may hold values from -0.25 to 0.25
- wannier_k: bfloat16 [128, 256], replicated, may hold values from -0.375 to 0.375
- wannier_kq: bfloat16 [8, 128, 256], replicated, may hold values from -0.375 to 0.375
Outputs:
- coupling: float32 [288, 8, 128, 256], P('lat', None, 'row')
All inputs are finite; a program needn't handle non-finite values.
Results may differ from a plain program's by a relative error of at most 0.024.
Values may be sent and summed in bfloat16 or wider, within the bound.
A program may use at most 64 MiB of HBM per device.

v0:
```python
import math

import jax
import jax.numpy as jnp
from jax import lax
from jax.sharding import PartitionSpec as P

FINE = 40


def phases(qgrid, lattice, degeneracy):
    product = jnp.sum(qgrid[:, None, :] * lattice[None, :, :], axis=-1) % FINE
    angle = 2.0 * math.pi / FINE * product.astype(jnp.float32)
    weight = 1.0 / degeneracy.astype(jnp.float32)
    return (jnp.cos(angle) * weight[None, :], jnp.sin(angle) * weight[None, :])


def per_device(g_wannier, lattice, degeneracy, qgrid, phonon_vectors, wannier_k, wannier_kq):
    local_r, modes, rows_m, wide = g_wannier.shape
    width = wide // 2
    points = qgrid.shape[0]
    cosines, sines = phases(qgrid, lattice, degeneracy)
    flat = g_wannier.reshape(local_r, modes * rows_m * wide).astype(jnp.float32)
    first = jnp.dot(cosines, flat, precision=lax.Precision.HIGHEST).reshape(
        points, modes, rows_m, 2, width
    )
    second = jnp.dot(sines, flat, precision=lax.Precision.HIGHEST).reshape(
        points, modes, rows_m, 2, width
    )
    real_part = first[:, :, :, 0] - second[:, :, :, 1]
    imag_part = first[:, :, :, 1] + second[:, :, :, 0]
    stacked = jnp.concatenate([real_part, imag_part], axis=1).reshape(
        points, 2 * modes, rows_m * width
    )
    stacked = stacked.astype(jnp.bfloat16)
    everyone = lax.all_gather(phonon_vectors, "lat", axis=1, tiled=True)
    er = everyone[:, :, :modes]
    ei = everyone[:, :, modes:]
    emat = jnp.stack([jnp.concatenate([er, -ei], -1), jnp.concatenate([ei, er], -1)], axis=2)
    branch_rows = phonon_vectors.shape[1]
    uk_real = wannier_k[:, :width]
    uk_imag = wannier_k[:, width:]
    right_mat = jnp.concatenate([wannier_k, jnp.concatenate([-uk_imag, uk_real], 1)], 0).reshape(
        2, width, wide
    )
    ur = wannier_kq[:, :, :width]
    ui = wannier_kq[:, :, width:]
    left_mat = jnp.stack([jnp.concatenate([ur, -ui], -1), jnp.concatenate([ui, ur], -1)], axis=1)
    summed = lax.psum_scatter(
        jnp.einsum("qvck,qkx->vqcx", emat, stacked, preferred_element_type=jnp.float32).astype(
            jnp.bfloat16
        ),
        "lat",
        scatter_dimension=0,
        tiled=True,
    ).astype(jnp.float32)
    finish_summed = summed
    finish_summed = finish_summed.astype(jnp.bfloat16).reshape(
        branch_rows, points, 2, rows_m, width
    )
    rotated = jnp.einsum(
        "vqcmn,cnx->vqmx", finish_summed, right_mat, preferred_element_type=jnp.float32
    )
    rotated, left_part = (
        rotated.astype(jnp.bfloat16).reshape(branch_rows, points, rows_m, 2, width),
        left_mat,
    )
    moved = lax.all_to_all(rotated, "row", split_axis=4, concat_axis=2, tiled=True)
    coupling = jnp.einsum("vqmcn,qcmx->vqnx", moved, left_part, preferred_element_type=jnp.float32)
    return coupling


def solution(mesh):
    in_specs = (
        P("lat", None, "row", None),
        P("lat", None),
        P("lat"),
        P(),
        P(None, "lat", None),
        P(),
        P(),
    )
    out_specs = P("lat", None, "row", None)
    return jax.shard_map(
        per_device, mesh=mesh, in_specs=in_specs, out_specs=out_specs, check_vma=False
    )
```

profile of v0, /device:TPU:1, one launch (start us, length us, event | category | flops | bytes accessed | tf_op | source)
XLA Modules:
  0.0 285.3 jit_solution(7168528969548537119)
XLA Ops:
  6.5 0.7 all-gather.2.cloned.1.call-update
  7.3 6.7 %reshape.30 = bf16[6,307200]{1,0:T(8,128)(2,1)} reshape(bf16[6,300,4,256]{3,2,1,0:T(4,128)(2,1)} %param.7) | data formatting | bytes 7372800 | tf_op jit(solution)/shard_map/reshape | solution.py:23
  14.1 6.9 %fusion.25 = f32[8,300,4,2,128]{4,0,3,2,1:T(8,128)S(1)} fusion(bf16[300,4,2,128,6]{3,4,2,1,0:T(8,128)(2,1)} %bitcast.78, s32[8,6]{1,0:T(8,128)S(1)} %multiply_reduce_fusion, f32[6]{0:T(128)S(1)} %convert_divide_fusion), kind=kOutput, calls=%fused_computation.35 | convolution fusion | flops 176947632 | bytes 13517016 | tf_op jit(solution)/shard_map/dot_general | solution.py:27
  21.0 4.3 %fusion.27 = f32[8,300,4,2,128]{4,0,3,2,1:T(8,128)S(1)} fusion(bf16[300,4,2,128,6]{3,4,2,1,0:T(8,128)(2,1)S(1)} %bitcast.79, s32[8,6]{1,0:T(8,128)S(1)} %multiply_reduce_fusion, f32[6]{0:T(128)S(1)} %convert_divide_fusion), kind=kOutput, calls=%fused_computation.37 | convolution fusion | flops 176947632 | bytes 13517016 | tf_op jit(solution)/shard_map/dot_general | solution.py:24
  25.3 1.4 fusion.10
  26.7 2.4 copy.45
  29.1 2.3 copy.46
  31.4 64.6 %all-gather.2.cloned.1.call-done = bf16[8,288,600]{2,0,1:T(8,128)(2,1)} async-done(((bf16[8,18,600]{2,0,1:T(8,128)(2,1)}), bf16[8,288,600]{2,0,1:T(8,128)(2,1)}) %all-gather.2.cloned.1.call-update) | async-done | bytes 2764816 | tf_op jit(solution)/shard_map/all_gather | solution.py:36
  96.0 3.0 %fusion.51 = (bf16[8,288,300]{2,0,1:T(8,128)(2,1)S(1)}, bf16[8,288,300]{2,0,1:T(8,128)(2,1)S(1)}) fusion(bf16[8,288,600]{2,0,1:T(8,128)(2,1)} %all-gather.2.cloned.1.call-done), kind=kLoop, calls=%fused_computation.62 | loop fusion | bytes 5529600 | tf_op jit(solution)/shard_map/slice | solution.py:38
  99.0 0.5 copy_negate_fusion
  99.7 4.2 %maximum_bitcast_fusion.2 = (bf16[8,288,1,600]{3,1,2,0:T(8,128)(2,1)S(1)}, bf16[8,288,1,600]{3,1,2,0:T(8,128)(2,1)}) fusion(bf16[8,288,300]{2,1,0:T(8,128)(2,1)S(1)} %get-tuple-element.11, bf16[8,288,300]{2,1,0:T(8,128)(2,1)S(1)} %copy.65, bf16[8,288,300]{2,1,0:T(8,128)(2,1)S(1)} %get-tuple-element.12), kind=kLoop, calls=%fused_computation.12 | loop fusion | flops 11059200 | bytes 9676800 | tf_op jit(solution)/shard_map/stack | solution.py:39
  104.0 9.3 %convert_bitcast_fusion = bf16[288,8,2,512]{3,0,2,1:T(8,128)(2,1)} fusion(bf16[8,288,1,600]{3,1,2,0:T(8,128)(2,1)} %get-tuple-element.10, bf16[8,288,1,600]{3,1,2,0:T(8,128)(2,1)S(1)} %get-tuple-element.9, bf16[8,300,512]{2,1,0:T(8,128)(2,1)} %copy.46, bf16[8,300,512]{2,1,0:T(8,128)(2,1)} %copy.45), kind=kOutput, calls=%fused_computation.11 | convolution fusion | flops 2854404096 | bytes 15163392 | tf_op jit(solution)/shard_map/qvck,qkx->vqcx/dot_general | solution.py:50
  113.3 7.2 %copy.50 = bf16[288,8,2,512]{3,1,2,0:T(8,128)(2,1)} copy(bf16[288,8,2,512]{3,0,2,1:T(8,128)(2,1)} %convert_bitcast_fusion) | data formatting | bytes 9437184 | tf_op jit(solution)/shard_map/convert_element_type | solution.py:50
  120.4 0.8 copy-done.2
  121.3 97.9 %reduce-scatter.2.cloned.1.call-done = bf16[18,8,2,512]{3,1,2,0:T(8,128)(2,1)} async-done(((bf16[288,8,2,512]{3,1,2,0:T(8,128)(2,1)}), bf16[18,8,2,512]{3,1,2,0:T(8,128)(2,1)}) %reduce-scatter.2.cloned.1.call-update) | async-done | bytes 294928 | tf_op jit(solution)/shard_map/reduce_scatter | solution.py:49
  219.2 1.3 fusion.18
  220.5 3.2 %copy.52 = bf16[18,8,4,2,128]{0,1,3,2,4:T(8,128)(2,1)S(1)} copy(bf16[18,8,4,2,128]{4,1,3,2,0:T(8,128)(2,1)S(1)} %fusion.18) | data formatting | bytes 589824 | tf_op jit(solution)/shard_map/reshape | solution.py:65
  223.7 4.6 %reshape.41 = bf16[32,2,2304]{2,1,0:T(2,128)(2,1)} reshape(bf16[128,4,2,8,18]{4,3,2,1,0:T(8,128)(2,1)S(1)} %bitcast.80) | data formatting | bytes 589824
  228.3 22.8 %all-to-all-start = ((bf16[32,2,2304]{2,1,0:T(2,128)(2,1)}), bf16[32,2,2304]{2,1,0:T(2,128)(2,1)S(1)}, u32[]{:S(2)}, u32[]{:S(2)}) async-start(bf16[32,2,2304]{2,1,0:T(2,128)(2,1)} %reshape.41), calls=%async_computation.1 | async-start | bytes 589824 | tf_op jit(solution)/shard_map/all_to_all | solution.py:68
  251.3 17.9 %all-to-all-done = bf16[32,2,2304]{2,1,0:T(2,128)(2,1)S(1)} async-done(((bf16[32,2,2304]{2,1,0:T(2,128)(2,1)}), bf16[32,2,2304]{2,1,0:T(2,128)(2,1)S(1)}, u32[]{:S(2)}, u32[]{:S(2)}) %all-to-all-start) | async-done | bytes 294944 | tf_op jit(solution)/shard_map/all_to_all | solution.py:68
  269.2 5.2 %reshape.42 = bf16[128,4,2,8,18]{4,3,2,1,0:T(8,128)(2,1)S(1)} reshape(bf16[32,2,2304]{2,1,0:T(2,128)(2,1)S(1)} %all-to-all-done) | data formatting | bytes 589824
  274.4 0.6 copy.54
  275.0 2.5 fusion.14
  277.4 1.0 copy.56
  (21 shorter events, 0.6 us)
Async XLA Ops:
  6.5 89.5 %all-gather.2.cloned.1.call-start = ((), (), s32[]{:S(2)}) async-start(), calls=%async_computation.2 | async-start | bytes 3133440 | tf_op jit(solution)/shard_map/all_gather | solution.py:36
  7.3 6.7 %copy-start.3 = (s32[6,3]{0,1:T(4,128)S(1)}, s32[6,3]{0,1:T(4,128)}, u32[]{:S(2)}) copy-start(s32[6,3]{0,1:T(4,128)} %param.8) | copy-start | bytes 220
  7.3 6.7 %copy-start.4 = (s32[8,3]{0,1:T(4,128)S(1)}, s32[8,3]{0,1:T(4,128)}, u32[]{:S(2)}) copy-start(s32[8,3]{0,1:T(4,128)} %param.10) | copy-start | bytes 292
  7.3 6.8 %copy-start.5 = (s32[6]{0:T(128)S(1)}, s32[6]{0:T(128)}, u32[]{:S(2)}) copy-start(s32[6]{0:T(128)} %param.9) | copy-start | bytes 76
  7.3 211.9 %reduce-scatter.2.cloned.1.call-start = ((), (), s32[]{:S(2)}) async-start(), calls=%async_computation.3 | async-start | bytes 5013504 | tf_op jit(solution)/shard_map/reduce_scatter | solution.py:49
  14.1 6.9 %copy-start = (bf16[6,307200]{1,0:T(8,128)(2,1)S(1)}, bf16[6,307200]{1,0:T(8,128)(2,1)}, u32[]{:S(2)}) copy-start(bf16[6,307200]{1,0:T(8,128)(2,1)} %reshape.30) | copy-start | bytes 11059204
  120.4 0.8 copy-start.2
  219.2 31.9 %copy-start.1 = (bf16[8,128,256]{2,1,0:T(8,128)(2,1)S(1)}, bf16[8,128,256]{2,1,0:T(8,128)(2,1)}, u32[]{:S(2)}) copy-start(bf16[8,128,256]{2,1,0:T(8,128)(2,1)} %param.13) | copy-start | bytes 1572868
  228.3 40.9 %all-to-all-start = ((bf16[32,2,2304]{2,1,0:T(2,128)(2,1)}), bf16[32,2,2304]{2,1,0:T(2,128)(2,1)S(1)}, u32[]{:S(2)}, u32[]{:S(2)}) async-start(bf16[32,2,2304]{2,1,0:T(2,128)(2,1)} %reshape.41), calls=%async_computation.1 | async-start | bytes 589824 | tf_op jit(solution)/shard_map/all_to_all | solution.py:68
Sparse Core Ops, SparseCore 0:
  9.4 86.5 all-gather.1
  120.6 98.6 reduce-scatter.1
where the time goes:
time: 286 us; the launch traced here: 285 us
  waiting for transfers between devices  181 us (63%)
  local copies, waits for them, and re-layouts  37.2 us (13%)
  matrix products  24.2 us (8%)
  starting transfers between devices  22.8 us (8%)
  between operations  13.6 us (5%)
  other arithmetic  6.38 us (2%)
    reduce_scatter x1, waiting for transfers between devices, per_device(): lax.psum_scatter(jnp.einsum('qvck,qkx->vqcx', emat, stacked, preferred_el...  97.9 us
    all_gather x1, waiting for transfers between devices, per_device(): everyone = lax.all_gather(phonon_vectors, 'lat', axis=1, tiled=True)  64.6 us
    all_to_all x1, starting transfers between devices, per_device(): lax.all_to_all(rotated, 'row', split_axis=4, concat_axis=2, tiled=True)  22.8 us
    all_to_all x1, waiting for transfers between devices, per_device(): lax.all_to_all(rotated, 'row', split_axis=4, concat_axis=2, tiled=True)  17.9 us
    unnamed x15, local copies, waits for them, and re-layouts  10.9 us
    dot_general x1, matrix products, per_device(): jnp.einsum('qvck,qkx->vqcx', emat, stacked, preferred_element_type=jnp.fl...  9.3 us
    convert_element_type x1, local copies, waits for them, and re-layouts, per_device(): jnp.einsum('qvck,qkx->vqcx', emat, stacked, preferred_element_type=jnp.fl...  7.16 us
    dot_general x1, matrix products, per_device(): jnp.dot(sines, flat, precision=lax.Precision.HIGHEST)  6.91 us
  transfers between devices with their start and end apart: 3, of which 3 were waited for; matrix products, arithmetic and copies ran while one was open for 8% of the time, Pallas kernels for 0%

commit v1 on v0

v1 whole, which is shorter than its diff:
```python
import functools
import math

import jax
import jax.numpy as jnp
from jax import lax
from jax.experimental import pallas as pl
from jax.experimental.pallas import tpu as pltpu
from jax.sharding import PartitionSpec as P

FINE = 40
NY = 4
NZ = 4
MESH = pl.DeviceIdType.MESH
F32 = jnp.float32
BF16 = jnp.bfloat16


def dot(a, b, contract=((1,), (0,))):
    return lax.dot_general(a, b, (contract, ((), ())), preferred_element_type=F32)


def times_i(x):
    half = x.shape[-1] // 2
    return jnp.concatenate([-x[:, half:], x[:, :half]], axis=1)


def kernel(rows, g_ref, a_ref, e_ref, rt_ref, l_ref, out_ref,
           part, yfar, ynear, e1, e2, e3, ef, eb, spart, zin, sfull, kt, kr, zf, ob, osend,
           yf_s, yf_r, yn_s, yn_r, e_s, e_r, z_s, z_r, row_s, row_r, o_s, o_r):
    n_lat, n_row = NY * NZ, rows
    lat = lax.axis_index("lat")
    row = lax.axis_index("row")
    y = lax.rem(lat, NY)
    z = lax.div(lat, NY)
    core = lax.rem(row, 2)
    n_r = g_ref.shape[1]
    modes = g_ref.shape[2]
    nv = e_ref.shape[1]
    vz = NY * nv

    def ypeer(d):
        return z * NY + lax.rem(y + d, NY)

    def zpeer(d):
        return lax.rem(z + d, NZ) * NY + y

    def remote(src, dst, ss, rs, **dev):
        return pltpu.make_async_remote_copy(
            src_ref=src, dst_ref=dst, send_sem=ss, recv_sem=rs, device_id=dev, device_id_type=MESH)

    barrier = pltpu.get_barrier_semaphore()
    for d in range(1, NY):
        pl.semaphore_signal(barrier, inc=1, device_id={"lat": ypeer(d)}, device_id_type=MESH)
    for d in range(1, NZ):
        pl.semaphore_signal(barrier, inc=1, device_id={"lat": zpeer(d)}, device_id_type=MESH)

    @pl.loop(1, n_row)
    def _(p):
        pl.semaphore_signal(barrier, inc=1, device_id={"row": lax.rem(row + p, n_row)}, device_id_type=MESH)

    pl.semaphore_wait(barrier, NY + NZ - 2 + n_row - 1)

    def e1_copy(d):
        yy = lax.rem(y + d, NY)
        return remote(e_ref.at[2 * yy + core], e1.at[y], e_s.at[d], e_r.at[y], lat=ypeer(d))

    def e1_in(d):
        yy = lax.rem(y + d, NY)
        return remote(e_ref.at[2 * yy + core], e1.at[yy], e_s.at[d], e_r.at[yy], lat=ypeer(d))

    def e2_copy(d):
        return remote(e1, e2.at[z], e_s.at[NY + d], e_r.at[NY + z], lat=zpeer(d))

    def e2_in(d):
        zz = lax.rem(z + d, NZ)
        return remote(e1, e2.at[zz], e_s.at[NY + d], e_r.at[NY + zz], lat=zpeer(d))

    def e3_copy():
        return remote(e2, e3, e_s.at[NY + NZ], e_r.at[NY + NZ], row=row + 1 - 2 * core)

    for d in range(1, NY):
        e1_copy(d).start()
    e1[y] = e_ref[2 * y + core]

    def phase_sums(m):
        for i in range(modes // 16):
            blocks = [g_ref[m, r, 16 * i:16 * i + 16, :] for r in range(n_r)]
            stack = jnp.concatenate(blocks + [times_i(b) for b in blocks], axis=0)
            res = dot(a_ref[...], stack).astype(BF16)
            for q in range(8):
                part[q, m, 16 * i:16 * i + 16, :] = res[16 * q:16 * q + 16, :]

    right, left = ypeer(1), ypeer(3)
    qa = 2 * lax.rem(y + 1, NY)
    qb = 2 * lax.rem(y + 2, NY)
    qc = 2 * lax.rem(y + 3, NY)

    def far(s, way):
        h, k = divmod(s, 2)
        return remote(part.at[qb + k, h + 2 * way], yfar.at[s, way], yf_s.at[s, way], yf_r.at[s, way],
                      lat=(right, left)[way])

    def near(s, way, half):
        h, k = divmod(s, 2)
        q = (qa, qc)[way] + k
        return remote(part.at[q, h + 2 * half], ynear.at[s, way, half], yn_s.at[s, way, half],
                      yn_r.at[s, way, half], lat=(right, left)[way])

    def start_far(s):
        for way in (0, 1):
            far(s, way).start()

    def start_own(s):
        for way in (0, 1):
            near(s, way, 1 - way).start()

    def start_sums(s):
        h, k = divmod(s, 2)
        for way in (0, 1):
            far(s, way).wait_recv()
            q = (qa, qc)[way] + k
            m = h + 2 * way
            part[q, m] = (part[q, m].astype(F32) + yfar[s, way].astype(F32)).astype(BF16)
            near(s, way, way).start()

    def branch(s):
        h, k = divmod(s, 2)
        for way in (0, 1):
            for half in (0, 1):
                near(s, way, half).wait_recv()
        res = []
        for half in (0, 1):
            total = (part[2 * y + k, h + 2 * half].astype(F32) + ynear[s, 0, half].astype(F32)
                     + ynear[s, 1, half].astype(F32)).astype(BF16)
            both = jnp.concatenate([total, times_i(total)], axis=0)
            res.append(dot(eb[k], both))
        for zz in range(NZ):
            spart[s, zz] = jnp.concatenate([r[vz * zz:vz * zz + vz] for r in res], axis=0).astype(BF16)
        for d in range(1, NZ):
            z_copy(s, d).start()

    def z_copy(s, d):
        return remote(spart.at[s, lax.rem(z + d, NZ)], zin.at[s, z], z_s.at[s, d], z_r.at[s, z], lat=zpeer(d))

    def z_in(s, d):
        zz = lax.rem(z + d, NZ)
        return remote(spart.at[s, zz], zin.at[s, zz], z_s.at[s, d], z_r.at[s, zz], lat=zpeer(d))

    def z_sum(s):
        h, k = divmod(s, 2)
        total = spart[s, z].astype(F32)
        for d in range(1, NZ):
            z_in(s, d).wait_recv()
            total = total + zin[s, lax.rem(z + d, NZ)].astype(F32)
        size = 2 * vz
        sfull[h, size * k:size * k + size, :] = total.astype(BF16)

    def row_copy(h, p):
        to = lax.rem(row + p, n_row)
        return remote(kt.at[h, to], kr.at[h, row], row_s.at[h, p], row_r.at[h, row], row=to)

    def row_in(h, p):
        other = lax.rem(row + p, n_row)
        return remote(kt.at[h, other], kr.at[h, other], row_s.at[h, p], row_r.at[h, other], row=other)

    def right_rotate(h):
        res = dot(rt_ref[...], sfull[h], ((1,), (1,)))
        kt[h] = res.reshape(kt.shape[1:]).astype(BF16)

        @pl.loop(1, n_row)
        def _(p):
            row_copy(h, p).start()

        kr[h, row] = kt[h, row]

    def left_rotate(h):
        @pl.loop(1, n_row)
        def _(p):
            row_in(h, p).wait_recv()

        tiles = zf.shape[0]
        got = kr[h].astype(F32).reshape(zf.shape[1], 128 * tiles)
        for t in range(tiles):
            zf[t] = got[:, 128 * t:128 * t + 128]
        for n in range(4):
            w = jnp.concatenate([zf[t, pl.ds(n, 2 * n_row, stride=4), :].T for t in range(tiles)], axis=0)
            for k in (0, 1):
                acc = None
                for half in (0, 1):
                    at = 2 * vz * k + vz * half
                    term = dot(w[at:at + vz].astype(BF16), l_ref[2 * y + k, h + 2 * half])
                    acc = term if acc is None else acc + term
                for t in range(2):
                    here = acc[:, 128 * t:128 * t + 128]
                    if h:
                        here = here + ob[k, t, pl.ds(n, vz, stride=4), :]
                    ob[k, t, pl.ds(n, vz, stride=4), :] = here

    sfull[:, 4 * vz:, :] = jnp.zeros((2, sfull.shape[1] - 4 * vz, sfull.shape[2]), BF16)
    phase_sums(0)
    phase_sums(2)
    start_far(0)
    start_own(0)
    start_far(1)
    for d in range(1, NY):
        e1_in(d).wait_recv()
    for d in range(1, NZ):
        e2_copy(d).start()
    e2[z] = e1[...]
    phase_sums(1)
    phase_sums(3)
    start_sums(0)
    start_own(1)
    start_far(2)
    for d in range(1, NZ):
        e2_in(d).wait_recv()
    e3_copy().start()
    for l in range(n_lat):
        ef[nv * l:nv * l + nv, :] = e2[l // NY, l % NY].astype(F32)
    eb[core] = ef[...].astype(BF16)
    e3_copy().wait_recv()
    for l in range(n_lat):
        ef[nv * l:nv * l + nv, :] = e3[l // NY, l % NY].astype(F32)
    eb[1 - core] = ef[...].astype(BF16)
    start_sums(1)
    start_own(2)
    start_far(3)
    branch(0)
    start_sums(2)
    start_own(3)
    z_sum(0)
    branch(1)
    start_sums(3)
    z_sum(1)
    right_rotate(0)
    branch(2)
    z_sum(2)
    branch(3)
    left_rotate(0)
    z_sum(3)
    right_rotate(1)
    left_rotate(1)

    def o_copy(d):
        return remote(osend.at[lax.rem(y + d, NY)], out_ref.at[y], o_s.at[d], o_r.at[y], lat=ypeer(d))

    def o_in(d):
        yy = lax.rem(y + d, NY)
        return remote(osend.at[yy], out_ref.at[yy], o_s.at[d], o_r.at[yy], lat=ypeer(d))

    size = 4 * nv
    for yy in range(NY):
        osend[yy] = jnp.concatenate(
            [jnp.concatenate([ob[k, t, size * yy:size * yy + size, :] for t in range(2)], axis=1) for k in (0, 1)],
            axis=0).astype(BF16)
    for d in range(1, NY):
        o_copy(d).start()
    out_ref[y] = osend[y]

    for d in range(1, NY):
        e1_copy(d).wait_send()
    for d in range(1, NZ):
        e2_copy(d).wait_send()
    e3_copy().wait_send()
    for s in range(4):
        for way in (0, 1):
            far(s, way).wait_send()
            for half in (0, 1):
                near(s, way, half).wait_send()
        for d in range(1, NZ):
            z_copy(s, d).wait_send()
    for h in (0, 1):
        @pl.loop(1, n_row)
        def _(p):
            row_copy(h, p).wait_send()
    for d in range(1, NY):
        o_in(d).wait_recv()
        o_copy(d).wait_send()


def phases(qgrid, lattice, degeneracy):
    product = jnp.sum(qgrid[:, None, :] * lattice[None, :, :], axis=-1) % FINE
    angle = 2.0 * math.pi / FINE * product.astype(F32)
    weight = 1.0 / degeneracy.astype(F32)
    return jnp.cos(angle) * weight[None, :], jnp.sin(angle) * weight[None, :]


def per_device(n_row, g_wannier, lattice, degeneracy, qgrid, phonon_vectors, wannier_k, wannier_kq):
    n_r, modes, rows_m, wide = g_wannier.shape
    width = wide // 2
    points, nv, _ = phonon_vectors.shape
    full = -(-modes // 16) * 16
    vz = NY * nv
    lanes = -(-4 * vz // 128) * 128

    cosines, sines = phases(qgrid, lattice, degeneracy)
    phase = jnp.concatenate([cosines, sines], axis=1).astype(BF16)
    a = (phase[:, None, :, None] * jnp.eye(16, dtype=BF16)[None, :, None, :]).reshape(points * 16, 2 * n_r * 16)
    g = jnp.pad(jnp.transpose(g_wannier, (2, 0, 1, 3)), ((0, 0), (0, 0), (0, full - modes), (0, 0)))
    e = jnp.pad(phonon_vectors.reshape(points, nv, 2, modes), ((0, 0), (0, 0), (0, 0), (0, full - modes)))
    e = e.reshape(points, nv, 2 * full)
    uk_real, uk_imag = wannier_k[:, :width], wannier_k[:, width:]
    right = jnp.concatenate([wannier_k, jnp.concatenate([-uk_imag, uk_real], 1)], 0)
    rt = right.T.reshape(2, n_row, width // n_row, wide).transpose(1, 0, 2, 3).reshape(wide, wide)
    ur, ui = wannier_kq[:, :, :width], wannier_kq[:, :, width:]
    left = jnp.stack([jnp.concatenate([ur, -ui], -1), jnp.concatenate([ui, ur], -1)], axis=1)
    left = left.reshape(points, 2, n_row, rows_m, wide).transpose(0, 3, 2, 1, 4).reshape(points, rows_m, 2 * n_row, wide)

    dma = pltpu.SemaphoreType.DMA
    vmem = pl.BlockSpec(memory_space=pltpu.VMEM)
    out = pl.pallas_call(
        functools.partial(kernel, n_row),
        out_shape=jax.ShapeDtypeStruct((NY, 8 * nv, wide), BF16),
        in_specs=[vmem] * 5,
        out_specs=vmem,
        scratch_shapes=[
            pltpu.VMEM((points, rows_m, full, wide), BF16),
            pltpu.VMEM((4, 2, full, wide), BF16),
            pltpu.VMEM((4, 2, 2, full, wide), BF16),
            pltpu.VMEM((NY, nv, 2 * full), BF16),
            pltpu.VMEM((NZ, NY, nv, 2 * full), BF16),
            pltpu.VMEM((NZ, NY, nv, 2 * full), BF16),
            pltpu.VMEM((NZ * vz, 2 * full), F32),
            pltpu.VMEM((2, NZ * vz, 2 * full), BF16),
            pltpu.VMEM((4, NZ, 2 * vz, wide), BF16),
            pltpu.VMEM((4, NZ, 2 * vz, wide), BF16),
            pltpu.VMEM((2, lanes, wide), BF16),
            pltpu.VMEM((2, n_row, wide // n_row, lanes), BF16),
            pltpu.VMEM((2, n_row, wide // n_row, lanes), BF16),
            pltpu.VMEM((lanes // 128, wide, 128), F32),
            pltpu.VMEM((2, 2, 4 * vz, width), F32),
            pltpu.VMEM((NY, 8 * nv, wide), BF16),
            dma((4, 2)), dma((4, 2)),
            dma((4, 2, 2)), dma((4, 2, 2)),
            dma((NY + NZ + 1,)), dma((NY + NZ + 1,)),
            dma((4, NZ)), dma((4, NZ)),
            dma((2, n_row)), dma((2, n_row)),
            dma((NY,)), dma((NY,)),
        ],
        compiler_params=pltpu.CompilerParams(
            collective_id=0, has_side_effects=True, vmem_limit_bytes=48 * 1024 * 1024),
        name="interpolate",
    )(g, a, e, rt, left)
    out = out.reshape(NY, 2, nv, 4, wide).transpose(2, 0, 1, 3, 4)
    return out.reshape(nv, points, 4, wide).astype(F32)


def solution(mesh):
    in_specs = (
        P("lat", None, "row", None),
        P("lat", None),
        P("lat"),
        P(),
        P(None, "lat", None),
        P(),
        P(),
    )
    out_specs = P("lat", None, "row", None)
    return jax.shard_map(
        functools.partial(per_device, mesh.shape["row"]),
        mesh=mesh, in_specs=in_specs, out_specs=out_specs, check_vma=False)
```

time: 286 us -> 111 us (0.39)
  the two profiles are of different devices: /device:TPU:1 before, /device:TPU:96 now
where the time goes in v1:
time: 111 us; the launch traced here: 110 us
  Pallas kernels  95.4 us (86%)
  local copies, waits for them, and re-layouts  11.8 us (11%)
  other arithmetic  2.97 us (3%)
    pallas_call x1, Pallas kernels, per_device(): pl.pallas_call(functools.partial(kernel, n_row), out_shape=jax.ShapeDtype...  95.4 us
    unnamed x15, local copies, waits for them, and re-layouts  4.62 us
    transpose x1, other arithmetic, per_device(): left.reshape(points, 2, n_row, rows_m, wide).transpose(0, 3, 2, 1, 4)  2.43 us
    another operation x4, local copies, waits for them, and re-layouts, per_device(): jnp.stack([jnp.concatenate([ur, -ui], -1), jnp.concatenate([ui, ur], -1)]...  2.27 us

profile of v1, /device:TPU:96, one launch (start us, length us, event | category | flops | bytes accessed | tf_op | source)
XLA Modules:
  0.0 110.4 jit_solution(1899323386449468652)
XLA Ops:
  0.0 2.5 %copy.36 = bf16[6,300,4,256]{3,1,0,2:T(8,128)(2,1)S(1)} copy(bf16[6,300,4,256]{3,2,1,0:T(4,128)(2,1)} %param.7) | data formatting | bytes 7372800 | tf_op args[0]
  2.6 2.1 %pad.8.g_ref = bf16[4,6,304,256]{3,2,1,0:T(8,128)(2,1)} pad(bf16[4,6,300,256]{3,2,1,0:T(8,128)(2,1)S(1)} %bitcast.18, bf16[]{:T(256)} %constant.14.clone.1), padding=0_0x0_0x0_4x0_0 | pad | bytes 7421954 | tf_op jit(solution)/shard_map/jit(_pad)/pad | solution.py:300
  4.7 0.1 multiply_reduce_fusion
  4.8 0.1 pad_maximum_fusion.2
  4.9 0.1 copy.27
  5.0 0.1 broadcast_multiply_fusion
  5.1 0.3 mul.69
  5.4 0.1 copy.32.a_ref
  5.5 0.2 reshape.64
  5.7 0.2 pad.9
  5.9 0.2 reshape.65
  6.2 0.1 copy.28
  6.5 0.1 slice_negate_fusion.1
  6.5 0.1 pad_maximum_fusion
  6.7 0.1 stack.10
  6.8 1.0 copy.31
  7.8 0.1 stack.9
  7.9 1.0 copy.30
  9.0 2.4 %maximum_bitcast_fusion = bf16[8,4,32,2,256]{4,3,2,1,0:T(2,128)(2,1)S(1)} fusion(bf16[8,1,32,4,256]{4,1,2,3,0:T(2,128)(2,1)S(1)} %copy.31, bf16[8,1,32,4,256]{4,1,2,3,0:T(2,128)(2,1)S(1)} %copy.30), kind=kLoop, calls=%fused_computation.1 | loop fusion | flops 2097152 | bytes 2097152 | tf_op jit(solution)/shard_map/transpose | solution.py:308
  11.4 0.4 reshape.68.l_ref
  11.9 2.0 %copy-done = bf16[4,6,304,256]{3,2,1,0:T(8,128)(2,1)S(1)} copy-done((bf16[4,6,304,256]{3,2,1,0:T(8,128)(2,1)S(1)}, bf16[4,6,304,256]{3,2,1,0:T(8,128)(2,1)}, u32[]{:S(2)}) %copy-start) | copy-done | bytes 3735576
  13.9 95.4 %interpolate.1 = bf16[4,144,256]{2,1,0:T(8,128)(2,1)S(1)} custom-call(bf16[4,6,304,256]{3,2,1,0:T(8,128)(2,1)S(1)} %copy-done, bf16[128,192]{1,0:T(8,128)(2,1)S(1)} %copy.32.a_ref, bf16[8,18,608]{2,1,0:T(8,128)(2,1)S(1)} %copy.33.e_ref, bf16[256,256]{1,0:T(8,128)(2,1)S(1)} %reshape.67.rt_ref, bf16[8,4,64,256]{3,2,1,0:T(8,128)(2,1)S(1)} %reshape.68.l_ref), custom_call_target="tpu_custom_call" | custom-call | tf_op jit(solution)/shard_map/interpolate/pallas_call | solution.py:312
  109.3 0.1 reshape.70
  109.5 1.0 copy.34
  (22 shorter events, 0.3 us)
Async XLA Ops:
  2.5 2.1 %copy-start.4 = (s32[6,3]{0,1:T(4,128)S(1)}, s32[6,3]{0,1:T(4,128)}, u32[]{:S(2)}) copy-start(s32[6,3]{0,1:T(4,128)} %param.8) | copy-start | bytes 220
  2.6 2.1 %copy-start.5 = (s32[8,3]{0,1:T(4,128)S(1)}, s32[8,3]{0,1:T(4,128)}, u32[]{:S(2)}) copy-start(s32[8,3]{0,1:T(4,128)} %param.10) | copy-start | bytes 292
  2.6 2.2 %copy-start.6 = (s32[6]{0:T(128)S(1)}, s32[6]{0:T(128)}, u32[]{:S(2)}) copy-start(s32[6]{0:T(128)} %param.9) | copy-start | bytes 76
  2.6 2.9 %copy-start.3 = (bf16[8,18,600]{2,0,1:T(8,128)(2,1)S(1)}, bf16[8,18,600]{2,0,1:T(8,128)(2,1)}, u32[]{:S(2)}) copy-start(bf16[8,18,600]{2,0,1:T(8,128)(2,1)} %param.11) | copy-start | bytes 518404
  2.6 3.6 %copy-start.2 = (bf16[128,256]{1,0:T(8,128)(2,1)S(1)}, bf16[128,256]{1,0:T(8,128)(2,1)}, u32[]{:S(2)}) copy-start(bf16[128,256]{1,0:T(8,128)(2,1)} %param.12) | copy-start | bytes 196612
  4.7 1.8 %copy-start.1 = (bf16[8,128,256]{2,1,0:T(8,128)(2,1)S(1)}, bf16[8,128,256]{2,1,0:T(8,128)(2,1)}, u32[]{:S(2)}) copy-start(bf16[8,128,256]{2,1,0:T(8,128)(2,1)} %param.13) | copy-start | bytes 1572868
  11.9 2.1 %copy-start = (bf16[4,6,304,256]{3,2,1,0:T(8,128)(2,1)S(1)}, bf16[4,6,304,256]{3,2,1,0:T(8,128)(2,1)}, u32[]{:S(2)}) copy-start(bf16[4,6,304,256]{3,2,1,0:T(8,128)(2,1)} %pad.8.g_ref) | copy-start | bytes 11206660

commit v2 on v1

v2 whole, which is shorter than its diff:
```python
import functools
import math

import jax
import jax.numpy as jnp
from jax import lax
from jax.experimental import pallas as pl
from jax.experimental.pallas import tpu as pltpu
from jax.sharding import PartitionSpec as P

FINE = 40
NY = 4
NZ = 4
MESH = pl.DeviceIdType.MESH
F32 = jnp.float32
BF16 = jnp.bfloat16


def dot(a, b, contract=((1,), (0,))):
    return lax.dot_general(a, b, (contract, ((), ())), preferred_element_type=F32)


def times_i(x):
    half = x.shape[-1] // 2
    return jnp.concatenate([-x[:, half:], x[:, :half]], axis=1)


def iota(shape, dim):
    return lax.broadcasted_iota(jnp.int32, shape, dim)


def one_hot(condition):
    return jnp.where(condition, 1.0, 0.0).astype(BF16)


UNITS = 8
COLUMN = (0, 72, 144, 216, 288, 360, 432, 512)
WINDOWS = ((0, 256), (256, 384), (384, 512), (512, 640))


def kernel(rows, g_ref, tail_ref, ph_ref, e_ref, wk_ref, wkq_ref, out_ref,
           part, yfar, ynear, e1, e2, e3, ef, eb, spart, zin_a, zmid, zin_b, sfull, rt, lf, lb,
           kt0, kt1, kt2, kt3, kr0, kr1, kr2, kr3, zf, ob, osend,
           yf_s, yf_r, yn_s, yn_r, e_s, e_r, za_s, za_r, zb_s, zb_r, row_s, row_r, o_s, o_r):
    n_row = rows
    kt, kr = (kt0, kt1, kt2, kt3), (kr0, kr1, kr2, kr3)
    lat = lax.axis_index("lat")
    row = lax.axis_index("row")
    y = lax.rem(lat, NY)
    z = lax.div(lat, NY)
    z_par, z_half = lax.rem(z, 2), lax.div(z, 2)
    core = lax.rem(row, 2)
    n_r, modes = g_ref.shape[1], g_ref.shape[2]
    full = part.shape[2]
    nv = e_ref.shape[1]
    vz = NY * nv

    def ypeer(d):
        return z * NY + lax.rem(y + d, NY)

    def zpeer(d):
        return lax.rem(z + d, NZ) * NY + y

    def remote(src, dst, ss, rs, **dev):
        return pltpu.make_async_remote_copy(
            src_ref=src, dst_ref=dst, send_sem=ss, recv_sem=rs, device_id=dev, device_id_type=MESH)

    barrier = pltpu.get_barrier_semaphore()
    for d in range(1, NY):
        pl.semaphore_signal(barrier, inc=1, device_id={"lat": ypeer(d)}, device_id_type=MESH)
    for d in range(1, NZ):
        pl.semaphore_signal(barrier, inc=1, device_id={"lat": zpeer(d)}, device_id_type=MESH)

    @pl.loop(1, n_row)
    def _(p):
        pl.semaphore_signal(barrier, inc=1, device_id={"row": lax.rem(row + p, n_row)}, device_id_type=MESH)

    spread_rows = one_hot((iota((128, 16), 0) >> 4) == iota((128, 16), 1))
    spread_cols = one_hot(iota((128, 32 * n_r), 0) == (iota((128, 32 * n_r), 1) >> 4))
    same = (iota((128, 32 * n_r), 0) & 15) == (iota((128, 32 * n_r), 1) & 15)
    a = jnp.where(same, dot(dot(spread_rows, ph_ref[...]).astype(BF16), spread_cols), 0.0).astype(BF16)

    def phase_sums(m):
        for i in range(full // 16):
            if 16 * i + 16 <= modes:
                blocks = [g_ref[m, r, 16 * i:16 * i + 16, :] for r in range(n_r)]
            else:
                blocks = [tail_ref[m, r] for r in range(n_r)]
            stack = jnp.concatenate(blocks + [times_i(b) for b in blocks], axis=0)
            res = dot(a, stack).astype(BF16)
            for q in range(8):
                part[q, m, 16 * i:16 * i + 16, :] = res[16 * q:16 * q + 16, :]

    def e1_copy(d):
        yy = lax.rem(y + d, NY)
        return remote(e_ref.at[2 * yy + core], e1.at[y], e_s.at[d], e_r.at[y], lat=ypeer(d))

    def e1_in(d):
        yy = lax.rem(y + d, NY)
        return remote(e_ref.at[2 * yy + core], e1.at[yy], e_s.at[d], e_r.at[yy], lat=ypeer(d))

    def e2_copy(d):
        return remote(e2.at[z], e2.at[z], e_s.at[NY + d], e_r.at[NY + z], lat=zpeer(d))

    def e2_in(d):
        zz = lax.rem(z + d, NZ)
        return remote(e2.at[zz], e2.at[zz], e_s.at[NY + d], e_r.at[NY + zz], lat=zpeer(d))

    def e3_copy():
        return remote(e2, e3, e_s.at[NY + NZ], e_r.at[NY + NZ], row=row + 1 - 2 * core)

    def eigenvectors(source, k):
        whole = jnp.concatenate([source[zz].astype(F32) for zz in range(NZ)], axis=0).astype(BF16)
        at = iota((2 * modes, 2 * full), 0)
        to = iota((2 * modes, 2 * full), 1)
        spread = one_hot(jnp.where(at < modes, at, at + full - modes) == to)
        eb[k] = dot(whole, spread).astype(BF16)

    right, left = ypeer(1), ypeer(3)
    qa = 2 * lax.rem(y + 1, NY)
    qb = 2 * lax.rem(y + 2, NY)
    qc = 2 * lax.rem(y + 3, NY)

    def ways(u):
        cut = (full // 2 + 15) // 16 * 16
        cut = cut if u % 2 == 0 else full - cut
        return pl.ds(0, cut), pl.ds(cut, full - cut)

    def far(u, way):
        m, k = divmod(u, 2)
        here = ways(u)[way]
        return remote(part.at[qb + k, m, here], yfar.at[u, here], yf_s.at[u, way], yf_r.at[u, way],
                      lat=(right, left)[way])

    def near(u, way, half):
        m, k = divmod(u, 2)
        here = ways(u)[half]
        q = (qa, qc)[way] + k
        return remote(part.at[q, m, here], ynear.at[u, way, here], yn_s.at[u, way, half],
                      yn_r.at[u, way, half], lat=(right, left)[way])

    def start_far(u):
        for way in (0, 1):
            far(u, way).start()

    def start_own(u):
        for way in (0, 1):
            near(u, way, 1 - way).start()

    def start_sums(u):
        m, k = divmod(u, 2)
        for way in (0, 1):
            far(u, way).wait_recv()
            q = (qa, qc)[way] + k
            here = ways(u)[way]
            part[q, m, here, :] = (part[q, m, here, :].astype(F32) + yfar[u, here, :].astype(F32)).astype(BF16)
            near(u, way, way).start()

    def z_copy_a(u):
        return remote(spart.at[u, 1 - z_par], zin_a.at[u], za_s.at[u], za_r.at[u],
                      lat=(z + 1 - 2 * z_par) * NY + y)

    def z_copy_b(u):
        return remote(zmid.at[u], zin_b.at[u], zb_s.at[u], zb_r.at[u], lat=zpeer(2))

    def branch(u):
        m, k = divmod(u, 2)
        for way in (0, 1):
            for half in (0, 1):
                near(u, way, half).wait_recv()
        total = (part[2 * y + k, m].astype(F32) + ynear[u, 0].astype(F32) + ynear[u, 1].astype(F32)).astype(BF16)
        res = dot(eb[k], jnp.concatenate([total, times_i(total)], axis=0))
        for zz in range(NZ):
            spart[u, zz % 2, zz // 2] = res[vz * zz:vz * zz + vz].astype(BF16)
        z_copy_a(u).start()

    def z_middle(u):
        z_copy_a(u).wait_recv()
        other = 1 - z_half
        zmid[u] = (spart[u, z_par, other].astype(F32) + zin_a[u, other].astype(F32)).astype(BF16)
        z_copy_b(u).start()

    def z_end(u):
        own = spart[u, z_par, z_half].astype(F32) + zin_a[u, z_half].astype(F32)
        z_copy_b(u).wait_recv()
        sfull[COLUMN[u]:COLUMN[u] + vz, :] = own + zin_b[u].astype(F32)

    def row_copy(w, p):
        to = lax.rem(row + p, n_row)
        return remote(kt[w].at[to], kr[w].at[row], row_s.at[w, p], row_r.at[w, row], row=to)

    def row_in(w, p):
        other = lax.rem(row + p, n_row)
        return remote(kt[w].at[other], kr[w].at[other], row_s.at[w, p], row_r.at[w, other], row=other)

    def right_rotate(w):
        lo, hi = WINDOWS[w]
        res = dot(rt[...], sfull[lo:hi, :].astype(BF16), ((1,), (1,)))
        kt[w][...] = res.reshape(kt[w].shape).astype(BF16)

        @pl.loop(1, n_row)
        def _(p):
            row_copy(w, p).start()

        kr[w][row] = kt[w][row]

    def row_wait(w):
        @pl.loop(1, n_row)
        def _(p):
            row_in(w, p).wait_recv()

        lo, hi = WINDOWS[w]
        got = kr[w][...].astype(F32).reshape(8 * n_row, hi - lo)
        for t in range((hi - lo) // 128):
            zf[lo // 128 + t] = got[:, 128 * t:128 * t + 128]

    def left_rotate(units, first):
        lo = COLUMN[units[0]] // 128
        hi = -(-(COLUMN[units[-1]] + vz) // 128)
        for n in range(4):
            w = jnp.concatenate(
                [jnp.concatenate([zf[t, pl.ds(n + 4 * c, n_row, stride=8), :] for c in (0, 1)], axis=0).T
                 for t in range(lo, hi)], axis=0)
            for k in (0, 1):
                acc = None
                for u in units:
                    if u % 2 == k:
                        at = COLUMN[u] - 128 * lo
                        term = dot(w[at:at + vz].astype(BF16), lb[u])
                        acc = term if acc is None else acc + term
                if acc is None:
                    continue
                for t in range(2):
                    here = acc[:, 128 * t:128 * t + 128]
                    if not first:
                        here = here + ob[k, t, pl.ds(n, vz, stride=4), :]
                    ob[k, t, pl.ds(n, vz, stride=4), :] = here

    def rotations():
        r, j = iota((256, 256), 0), iota((256, 256), 1)
        perm = one_hot(j == ((r >> 2) & 1) * 128 + (r >> 3) * 4 + (r & 3))
        both = jnp.concatenate([wk_ref[...], times_i(wk_ref[...])], axis=0)
        rt[...] = dot(perm, both, ((1,), (1,))).astype(BF16)
        for k in (0, 1):
            for t in (0, 1):
                lf[k, t] = wkq_ref[2 * y + k, :, 128 * t:128 * t + 128].astype(F32)
        for u in range(UNITS):
            m, k = divmod(u, 2)
            ur = lf[k, 0, pl.ds(m, n_row, stride=4), :]
            ui = lf[k, 1, pl.ds(m, n_row, stride=4), :]
            lb[u] = jnp.concatenate([jnp.concatenate([ur, -ui], axis=1), jnp.concatenate([ui, ur], axis=1)],
                                    axis=0).astype(BF16)
        sfull[COLUMN[6] + vz:COLUMN[7], :] = jnp.zeros((COLUMN[7] - COLUMN[6] - vz, 256), F32)
        sfull[COLUMN[7] + vz:, :] = jnp.zeros((640 - COLUMN[7] - vz, 256), F32)

    pl.semaphore_wait(barrier, NY + NZ - 2 + n_row - 1)
    for d in range(1, NY):
        e1_copy(d).start()
    phase_sums(0)
    start_far(0)
    start_own(0)
    start_far(1)
    phase_sums(1)
    e1[y] = e_ref[2 * y + core]
    for d in range(1, NY):
        e1_in(d).wait_recv()
    for yy in range(NY):
        ef[nv * yy:nv * yy + nv, :] = e1[yy].astype(F32)
    e2[z] = ef[...].astype(BF16)
    for d in range(1, NZ):
        e2_copy(d).start()
    start_sums(0)
    start_own(1)
    start_far(2)
    phase_sums(2)
    start_sums(1)
    start_own(2)
    start_far(3)
    phase_sums(3)
    rotations()
    start_sums(2)
    start_own(3)
    start_far(4)
    for d in range(1, NZ):
        e2_in(d).wait_recv()
    e3_copy().start()
    eigenvectors(e2, core)
    start_sums(3)
    start_own(4)
    start_far(5)
    e3_copy().wait_recv()
    eigenvectors(e3, 1 - core)
    branch(0)
    branch(1)
    start_sums(4)
    start_own(5)
    start_far(6)
    z_middle(0)
    branch(2)
    z_middle(1)
    branch(3)
    z_end(0)
    start_sums(5)
    start_own(6)
    start_far(7)
    z_end(1)
    z_middle(2)
    z_middle(3)
    branch(4)
    z_end(2)
    z_end(3)
    right_rotate(0)
    start_sums(6)
    start_own(7)
    z_middle(4)
    branch(5)
    z_end(4)
    start_sums(7)
    z_middle(5)
    branch(6)
    z_end(5)
    right_rotate(1)
    z_middle(6)
    branch(7)
    z_end(6)
    right_rotate(2)
    z_middle(7)
    row_wait(0)
    row_wait(1)
    z_end(7)
    right_rotate(3)
    row_wait(2)
    left_rotate(range(7), True)
    row_wait(3)
    left_rotate((7,), False)

    def o_copy(d):
        return remote(osend.at[lax.rem(y + d, NY)], out_ref.at[y], o_s.at[d], o_r.at[y], lat=ypeer(d))

    def o_in(d):
        yy = lax.rem(y + d, NY)
        return remote(osend.at[yy], out_ref.at[yy], o_s.at[d], o_r.at[yy], lat=ypeer(d))

    size = 4 * nv
    for yy in range(NY):
        osend[yy] = jnp.concatenate(
            [jnp.concatenate([ob[k, t, size * yy:size * yy + size, :] for t in range(2)], axis=1) for k in (0, 1)],
            axis=0).astype(BF16)
    for d in range(1, NY):
        o_copy(d).start()
    out_ref[y] = osend[y]

    for d in range(1, NY):
        e1_copy(d).wait_send()
    for d in range(1, NZ):
        e2_copy(d).wait_send()
    e3_copy().wait_send()
    for u in range(UNITS):
        for way in (0, 1):
            far(u, way).wait_send()
            for half in (0, 1):
                near(u, way, half).wait_send()
        z_copy_a(u).wait_send()
        z_copy_b(u).wait_send()
    for w in range(len(WINDOWS)):
        @pl.loop(1, n_row)
        def _(p):
            row_copy(w, p).wait_send()
    for d in range(1, NY):
        o_in(d).wait_recv()
        o_copy(d).wait_send()


def phases(qgrid, lattice, degeneracy):
    product = jnp.sum(qgrid[:, None, :] * lattice[None, :, :], axis=-1) % FINE
    angle = 2.0 * math.pi / FINE * product.astype(F32)
    weight = 1.0 / degeneracy.astype(F32)
    return jnp.cos(angle) * weight[None, :], jnp.sin(angle) * weight[None, :]


def per_device(n_row, g_wannier, lattice, degeneracy, qgrid, phonon_vectors, wannier_k, wannier_kq):
    n_r, modes, rows_m, wide = g_wannier.shape
    width = wide // 2
    points, nv, _ = phonon_vectors.shape
    full = -(-modes // 16) * 16
    vz = NY * nv

    cosines, sines = phases(qgrid, lattice, degeneracy)
    phase = jnp.concatenate([cosines, sines], axis=1).astype(BF16)
    phase = jnp.pad(phase, ((0, 16 - points), (0, 128 - 2 * n_r)))
    g = jnp.transpose(g_wannier, (2, 0, 1, 3))
    tail = jnp.pad(g[:, :, full - 16:], ((0, 0), (0, 0), (0, full - modes), (0, 0)))

    dma = pltpu.SemaphoreType.DMA
    vmem = pl.BlockSpec(memory_space=pltpu.VMEM)
    widths = [hi - lo for lo, hi in WINDOWS]
    out = pl.pallas_call(
        functools.partial(kernel, n_row),
        out_shape=jax.ShapeDtypeStruct((NY, 8 * nv, wide), BF16),
        in_specs=[vmem] * 6,
        out_specs=vmem,
        scratch_shapes=[
            pltpu.VMEM((points, rows_m, full, wide), BF16),
            pltpu.VMEM((UNITS, full, wide), BF16),
            pltpu.VMEM((UNITS, 2, full, wide), BF16),
            pltpu.VMEM((NY, nv, 2 * modes), BF16),
            pltpu.VMEM((NZ, vz, 2 * modes), BF16),
            pltpu.VMEM((NZ, vz, 2 * modes), BF16),
            pltpu.VMEM((vz, 2 * modes), F32),
            pltpu.VMEM((2, NZ * vz, 2 * full), BF16),
            pltpu.VMEM((UNITS, 2, 2, vz, wide), BF16),
            pltpu.VMEM((UNITS, 2, vz, wide), BF16),
            pltpu.VMEM((UNITS, vz, wide), BF16),
            pltpu.VMEM((UNITS, vz, wide), BF16),
            pltpu.VMEM((WINDOWS[-1][1], wide), F32),
            pltpu.VMEM((wide, wide), BF16),
            pltpu.VMEM((2, 2, width, width), F32),
            pltpu.VMEM((UNITS, 2 * n_row, wide), BF16),
            *[pltpu.VMEM((n_row, wide // n_row, w), BF16) for w in widths],
            *[pltpu.VMEM((n_row, wide // n_row, w), BF16) for w in widths],
            pltpu.VMEM((WINDOWS[-1][1] // 128, wide, 128), F32),
            pltpu.VMEM((2, 2, 4 * vz, width), F32),
            pltpu.VMEM((NY, 8 * nv, wide), BF16),
            dma((UNITS, 2)), dma((UNITS, 2)),
            dma((UNITS, 2, 2)), dma((UNITS, 2, 2)),
            dma((NY + NZ + 1,)), dma((NY + NZ + 1,)),
            dma((UNITS,)), dma((UNITS,)), dma((UNITS,)), dma((UNITS,)),
            dma((len(WINDOWS), n_row)), dma((len(WINDOWS), n_row)),
            dma((NY,)), dma((NY,)),
        ],
        compiler_params=pltpu.CompilerParams(
            collective_id=0, has_side_effects=True, vmem_limit_bytes=36 * 1024 * 1024),
        name="interpolate",
    )(g, tail, phase, phonon_vectors, wannier_k, wannier_kq)
    out = out.reshape(NY, 2, nv, 4, wide).transpose(2, 0, 1, 3, 4)
    return out.reshape(nv, points, 4, wide).astype(F32)


def solution(mesh):
    in_specs = (
        P("lat", None, "row", None),
        P("lat", None),
        P("lat"),
        P(),
        P(None, "lat", None),
        P(),
        P(),
    )
    out_specs = P("lat", None, "row", None)
    return jax.shard_map(
        functools.partial(per_device, mesh.shape["row"]),
        mesh=mesh, in_specs=in_specs, out_specs=out_specs, check_vma=False)
```

time: 111 us -> 100 us (0.901)
  the two profiles are of different devices: /device:TPU:96 before, /device:TPU:1 now
where the time goes in v2:
time: 100 us
  Pallas kernels  93.8 us (94%)
  local copies, waits for them, and re-layouts  4.71 us (5%)
  other arithmetic  1.57 us (2%)
    pallas_call x1, Pallas kernels, per_device(): pl.pallas_call(functools.partial(kernel, n_row), out_shape=jax.ShapeDtype...  93.8 us
    unnamed x6, local copies, waits for them, and re-layouts  3.56 us

profile of v2, /device:TPU:1, one launch (start us, length us, event | category | flops | bytes accessed | tf_op | source)
XLA Modules:
  0.0 100.2 jit_solution(9567495491762537151)
XLA Ops:
  0.0 0.7 convert_divide_fusion
  0.7 0.8 multiply_reduce_fusion
  1.4 0.1 multiply_convert_fusion.1
  1.5 0.1 fusion.7.ph_ref
  1.6 1.0 copy.14.e_ref
  2.5 0.0 copy-start
  2.5 0.0 copy-start.1
  2.6 2.6 %copy.17 = bf16[6,300,4,256]{3,1,0,2:T(8,128)(2,1)S(1)} copy(bf16[6,300,4,256]{3,2,1,0:T(4,128)(2,1)} %param.7) | data formatting | bytes 7372800 | tf_op args[0]
  5.2 0.0 copy-done
  5.2 0.0 copy-done.1
  5.2 93.8 %interpolate.1 = bf16[4,144,256]{2,1,0:T(8,128)(2,1)S(1)} custom-call(bf16[4,6,300,256]{3,2,1,0:T(8,128)(2,1)S(1)} %bitcast.6, bf16[4,6,16,256]{3,2,1,0:T(8,128)(2,1)S(1)} %pad.8.tail_ref, bf16[16,128]{1,0:T(8,128)(2,1)S(1)} %fusion.7.ph_ref, bf16[8,18,600]{2,1,0:T(8,128)(2,1)S(1)} %copy.14.e_ref, bf16[128,256]{1,0:T(8,128)(2,1)S(1)} %copy-done.1, ...), custom_call_target="tpu_custom_call" | custom-call | tf_op jit(solution)/shard_map/interpolate/pallas_call | solution.py:397
  99.1 0.1 reshape.10
  99.2 1.0 copy.15
  (2 shorter events, 0.0 us)
Async XLA Ops:
  2.5 2.7 %copy-start = (bf16[8,128,256]{2,1,0:T(8,128)(2,1)S(1)}, bf16[8,128,256]{2,1,0:T(8,128)(2,1)}, u32[]{:S(2)}) copy-start(bf16[8,128,256]{2,1,0:T(8,128)(2,1)} %wkq_ref.1) | copy-start | bytes 1572868
  2.5 2.7 %copy-start.1 = (bf16[128,256]{1,0:T(8,128)(2,1)S(1)}, bf16[128,256]{1,0:T(8,128)(2,1)}, u32[]{:S(2)}) copy-start(bf16[128,256]{1,0:T(8,128)(2,1)} %wk_ref.1) | copy-start | bytes 196612

commit v3 on v2

v3 whole, which is shorter than its diff:
```python
import functools
import math

import jax
import jax.numpy as jnp
from jax import lax
from jax.experimental import pallas as pl
from jax.experimental.pallas import tpu as pltpu
from jax.sharding import PartitionSpec as P

FINE = 40
NY = 4
NZ = 4
NH = 4
MESH = pl.DeviceIdType.MESH
F32 = jnp.float32
BF16 = jnp.bfloat16


def dot(a, b, contract=((1,), (0,))):
    return lax.dot_general(a, b, (contract, ((), ())), preferred_element_type=F32)


def times_i(x):
    half = x.shape[-1] // 2
    return jnp.concatenate([-x[:, half:], x[:, :half]], axis=1)


def iota(shape, dim):
    return lax.broadcasted_iota(jnp.int32, shape, dim)


def one_hot(condition):
    return jnp.where(condition, 1.0, 0.0).astype(BF16)


UNITS = 8
COLUMN = (0, 72, 144, 216, 288, 360, 432, 512)
WINDOWS = ((0, 256), (256, 384), (384, 512), (512, 640))


def kernel(rows, g_ref, tail_ref, lattice_ref, degeneracy_ref, q_ref, e_ref, wk_ref, wkq_ref, out_ref,
           part, yfar, ynear, e0, e1, e2, e3, ef, eb, spart, zin, sfull, rt, lf, lb,
           kt0, kt1, kt2, kt3, km0, km1, km2, km3, kr0, kr1, kr2, kr3, zf, ob, osend,
           y_s, yf_r, yn_r, e_s, e_r, z_s, z_r, near_z, r1_s, r1_r, r2_s, r2_r, o_s, o_r):
    n_row = rows
    kt, km, kr = (kt0, kt1, kt2, kt3), (km0, km1, km2, km3), (kr0, kr1, kr2, kr3)
    lat = lax.axis_index("lat")
    row = lax.axis_index("row")
    y = lax.rem(lat, NY)
    z = lax.div(lat, NY)
    core = lax.rem(row, 2)
    n_xc = n_row // NH
    zh, xc = lax.div(row, n_xc), lax.rem(row, n_xc)
    n_r, modes = g_ref.shape[1], g_ref.shape[2]
    full = part.shape[2]
    nv = e_ref.shape[0]
    vz = NY * nv

    def ypeer(d):
        return z * NY + lax.rem(y + d, NY)

    def zpeer(d):
        return lax.rem(z + d, NZ) * NY + y

    def zh_peer(d):
        return lax.rem(row + n_xc * d, n_row)

    def xc_peer(p):
        return zh * n_xc + lax.rem(xc + p, n_xc)

    def remote(src, dst, ss, rs, **dev):
        return pltpu.make_async_remote_copy(
            src_ref=src, dst_ref=dst, send_sem=ss, recv_sem=rs, device_id=dev, device_id_type=MESH)

    barrier = pltpu.get_barrier_semaphore()
    for d in range(1, NY):
        pl.semaphore_signal(barrier, inc=1, device_id={"lat": ypeer(d)}, device_id_type=MESH)
    for d in range(1, NZ):
        pl.semaphore_signal(barrier, inc=1, device_id={"lat": zpeer(d)}, device_id_type=MESH)

    for d in (1, NH - 1):
        pl.semaphore_signal(barrier, inc=1, device_id={"row": zh_peer(d)}, device_id_type=MESH)

    @pl.loop(1, n_xc)
    def _(p):
        pl.semaphore_signal(barrier, inc=1, device_id={"row": xc_peer(p)}, device_id_type=MESH)

    at_q, at_r = iota((16, 128), 0), iota((16, 128), 1)
    is_cos = at_r < n_r
    at_r = jnp.where(is_cos, at_r, at_r - n_r)
    product = jnp.zeros((16, 128), jnp.int32)
    weight = jnp.ones((16, 128), jnp.int32)
    for r in range(n_r):
        column = jnp.zeros((16, 128), jnp.int32)
        for q in range(8):
            whole = sum(q_ref[c, q] * lattice_ref[c, r] for c in range(3))
            column = jnp.where(at_q == q, lax.rem(lax.rem(whole, FINE) + FINE, FINE), column)
        product = jnp.where(at_r == r, column, product)
        weight = jnp.where(at_r == r, degeneracy_ref[r], weight)
    angle = 2.0 * math.pi / FINE * product.astype(F32)
    phase = jnp.where(is_cos, jnp.cos(angle), jnp.sin(angle)) / weight.astype(F32)
    phase = jnp.where((at_r < n_r) & (at_q < 8), phase, 0.0).astype(BF16)

    spread_rows = one_hot((iota((128, 16), 0) >> 4) == iota((128, 16), 1))
    spread_cols = one_hot(iota((128, 32 * n_r), 0) == (iota((128, 32 * n_r), 1) >> 4))
    same = (iota((128, 32 * n_r), 0) & 15) == (iota((128, 32 * n_r), 1) & 15)
    a = jnp.where(same, dot(dot(spread_rows, phase).astype(BF16), spread_cols), 0.0).astype(BF16)

    def phase_sums(m):
        for i in range(full // 16):
            if 16 * i + 16 <= modes:
                blocks = [g_ref[m, r, 16 * i:16 * i + 16, :] for r in range(n_r)]
            else:
                blocks = [tail_ref[m, r] for r in range(n_r)]
            stack = jnp.concatenate(blocks + [times_i(b) for b in blocks], axis=0)
            res = dot(a, stack).astype(BF16)
            for q in range(8):
                part[q, m, 16 * i:16 * i + 16, :] = res[16 * q:16 * q + 16, :]

    def e1_copy(d):
        yy = lax.rem(y + d, NY)
        return remote(e0.at[yy], e1.at[y], e_s.at[d], e_r.at[y], lat=ypeer(d))

    def e1_in(d):
        yy = lax.rem(y + d, NY)
        return remote(e0.at[yy], e1.at[yy], e_s.at[d], e_r.at[yy], lat=ypeer(d))

    def e2_copy(d):
        return remote(e2.at[z], e2.at[z], e_s.at[NY + d], e_r.at[NY + z], lat=zpeer(d))

    def e2_in(d):
        zz = lax.rem(z + d, NZ)
        return remote(e2.at[zz], e2.at[zz], e_s.at[NY + d], e_r.at[NY + zz], lat=zpeer(d))

    def e3_copy():
        return remote(e2, e3, e_s.at[NY + NZ], e_r.at[NY + NZ], row=row + 1 - 2 * core)

    def pick():
        rows_in, rows_out = 8 * nv, NY * nv
        at, to = iota((rows_out, rows_in), 0), iota((rows_out, rows_in), 1)
        wanted = to & 7
        chosen = jnp.zeros((rows_out, rows_in), jnp.bool_)
        for yy in range(NY):
            chosen = chosen | ((at - nv * yy == (to >> 3)) & (wanted == 2 * yy + core))
        both = e_ref[...].astype(F32).reshape(rows_in, 2 * modes).astype(BF16)
        res = dot(one_hot(chosen), both)
        for yy in range(NY):
            e0[yy] = res[nv * yy:nv * yy + nv].astype(BF16)

    def eigenvectors(source, k):
        whole = jnp.concatenate([source[zz].astype(F32) for zz in range(NZ)], axis=0).astype(BF16)
        at = iota((2 * modes, 2 * full), 0)
        to = iota((2 * modes, 2 * full), 1)
        spread = one_hot(jnp.where(at < modes, at, at + full - modes) == to)
        eb[k] = dot(whole, spread).astype(BF16)

    right, left = ypeer(1), ypeer(3)
    qa = 2 * lax.rem(y + 1, NY)
    qb = 2 * lax.rem(y + 2, NY)
    qc = 2 * lax.rem(y + 3, NY)

    def ways(u):
        cut = (full // 2 + 15) // 16 * 16
        cut = cut if u % 2 == 0 else full - cut
        return pl.ds(0, cut), pl.ds(cut, full - cut)

    def far(u, way):
        k, m = divmod(u, 4)
        here = ways(u)[way]
        return remote(part.at[qb + k, m, here], yfar.at[u, here], y_s.at[u], yf_r.at[u, way],
                      lat=(right, left)[way])

    def near(u, way, half):
        k, m = divmod(u, 4)
        here = ways(u)[half]
        q = (qa, qc)[way] + k
        return remote(part.at[q, m, here], ynear.at[u, way, here], y_s.at[u],
                      yn_r.at[u], lat=(right, left)[way])

    def start_far(u):
        for way in (0, 1):
            far(u, way).start()

    def start_own(u):
        for way in (0, 1):
            near(u, way, 1 - way).start()

    def start_sums(u):
        k, m = divmod(u, 4)
        for way in (0, 1):
            far(u, way).wait_recv()
            q = (qa, qc)[way] + k
            here = ways(u)[way]
            part[q, m, here, :] = (part[q, m, here, :].astype(F32) + yfar[u, here, :].astype(F32)).astype(BF16)
            near(u, way, way).start()

    def z_copy(u, d):
        return remote(spart.at[u, lax.rem(z + d, NZ)], zin.at[u, z], z_s, z_r.at[u], lat=zpeer(d))

    def z_all(u):
        return remote(spart.at[u, 0:NZ - 1], zin.at[u, 0:NZ - 1], z_s, z_r.at[u], lat=zpeer(1))

    def branch(u):
        k, m = divmod(u, 4)
        remote(part.at[0:2, m], ynear.at[u], y_s.at[u], yn_r.at[u], lat=right).wait_recv()
        total = (part[2 * y + k, m].astype(F32) + ynear[u, 0].astype(F32) + ynear[u, 1].astype(F32)).astype(BF16)
        res = dot(eb[k], jnp.concatenate([total, times_i(total)], axis=0))
        for zz in range(NZ):
            spart[u, zz] = res[vz * zz:vz * zz + vz].astype(BF16)
        for d in range(1, NZ):
            z_copy(u, d).start()

    def z_sum(u):
        z_all(u).wait_recv()
        total = spart[u, z].astype(F32)
        for d in range(1, NZ):
            total = total + zin[u, lax.rem(z + d, NZ)].astype(F32)
        sfull[COLUMN[u]:COLUMN[u] + vz, :] = total

    def step1(w, d):
        to = lax.rem(zh + d, NH)
        return remote(kt[w].at[to], km[w].at[zh], r1_s.at[w], r1_r.at[w], row=zh_peer(d))

    def step1_all(w):
        return remote(kt[w].at[0:NH - 1], km[w].at[0:NH - 1], r1_s.at[w], r1_r.at[w], row=zh_peer(1))

    def step2(w, p):
        return remote(km[w].at[:, lax.rem(xc + p, n_xc)], kr[w].at[:, xc], r2_s.at[w], r2_r.at[w], row=xc_peer(p))

    def step2_all(w):
        return remote(km[w].at[:, 0:n_xc - 1], kr[w].at[:, 0:n_xc - 1], r2_s.at[w], r2_r.at[w], row=xc_peer(1))

    def right_rotate(w):
        lo, hi = WINDOWS[w]
        res = dot(rt[...], sfull[lo:hi, :].astype(BF16), ((1,), (1,)))
        kt[w][...] = res.reshape(kt[w].shape).astype(BF16)
        for d in (2, 1, 3):
            step1(w, d).start()
        km[w][zh] = kt[w][zh]

    def row_forward(w):
        step1_all(w).wait_recv()

        @pl.loop(1, n_xc)
        def _(p):
            step2(w, p).start()

        for i in range(NH):
            kr[w][i, xc] = km[w][i, xc]

    def row_wait(w):
        step2_all(w).wait_recv()
        lo, hi = WINDOWS[w]
        got = kr[w][...].astype(F32).reshape(8 * n_row, hi - lo)
        for t in range((hi - lo) // 128):
            zf[lo // 128 + t] = got[:, 128 * t:128 * t + 128]

    def left_rotate(units, first):
        lo = COLUMN[units[0]] // 128
        hi = -(-(COLUMN[units[-1]] + vz) // 128)
        for n in range(4):
            w = jnp.concatenate(
                [jnp.concatenate([zf[t, pl.ds(n + 4 * c, n_row, stride=8), :] for c in (0, 1)], axis=0).T
                 for t in range(lo, hi)], axis=0)
            k = units[0] // 4
            acc = None
            for u in units:
                at = COLUMN[u] - 128 * lo
                term = dot(w[at:at + vz].astype(BF16), lb[u])
                acc = term if acc is None else acc + term
            for t in range(2):
                here = acc[:, 128 * t:128 * t + 128]
                if not first:
                    here = here + ob[k, t, pl.ds(n, vz, stride=4), :]
                ob[k, t, pl.ds(n, vz, stride=4), :] = here

    def o_copy(k, d):
        return remote(osend.at[k, lax.rem(y + d, NY)], out_ref.at[y, k], o_s.at[k, d], o_r.at[k, y], lat=ypeer(d))

    def o_in(k, d):
        yy = lax.rem(y + d, NY)
        return remote(osend.at[k, yy], out_ref.at[yy, k], o_s.at[k, d], o_r.at[k, yy], lat=ypeer(d))

    def send_result(k):
        size = 4 * nv
        for yy in range(NY):
            osend[k, yy] = jnp.concatenate(
                [ob[k, t, size * yy:size * yy + size, :] for t in range(2)], axis=1).astype(BF16)
        for d in (2, 1, 3):
            o_copy(k, d).start()
        out_ref[y, k] = osend[k, y]

    def rotations():
        r, j = iota((256, 256), 0), iota((256, 256), 1)
        perm = one_hot(j == ((r >> 2) & 1) * 128 + (r >> 3) * 4 + (r & 3))
        both = jnp.concatenate([wk_ref[...], times_i(wk_ref[...])], axis=0)
        rt[...] = dot(perm, both, ((1,), (1,))).astype(BF16)
        for k in (0, 1):
            for t in (0, 1):
                lf[k, t] = wkq_ref[2 * y + k, :, 128 * t:128 * t + 128].astype(F32)
        for u in range(UNITS):
            k, m = divmod(u, 4)
            ur = lf[k, 0, pl.ds(m, n_row, stride=4), :]
            ui = lf[k, 1, pl.ds(m, n_row, stride=4), :]
            lb[u] = jnp.concatenate([jnp.concatenate([ur, -ui], axis=1), jnp.concatenate([ui, ur], axis=1)],
                                    axis=0).astype(BF16)
        sfull[COLUMN[6] + vz:COLUMN[7], :] = jnp.zeros((COLUMN[7] - COLUMN[6] - vz, 256), F32)
        sfull[COLUMN[7] + vz:, :] = jnp.zeros((640 - COLUMN[7] - vz, 256), F32)

    pl.semaphore_wait(barrier, NY + NZ - 2 + 2 + n_xc - 1)
    pl.semaphore_signal(near_z, inc=1, device_id={"row": zh_peer(1)}, device_id_type=MESH)
    phase_sums(0)
    start_far(0)
    start_own(0)
    pick()
    for d in range(1, NY):
        e1_copy(d).start()
    e1[y] = e0[y]
    phase_sums(1)
    start_far(1)
    start_sums(0)
    start_own(1)
    phase_sums(2)
    start_far(2)
    for d in range(1, NY):
        e1_in(d).wait_recv()
    for yy in range(NY):
        ef[nv * yy:nv * yy + nv, :] = e1[yy].astype(F32)
    e2[z] = ef[...].astype(BF16)
    for d in range(1, NZ):
        e2_copy(d).start()
    start_sums(1)
    start_own(2)
    phase_sums(3)
    start_far(3)
    rotations()
    start_sums(2)
    start_own(3)
    start_far(4)
    for d in range(1, NZ):
        e2_in(d).wait_recv()
    e3_copy().start()
    eigenvectors(e2, core)
    start_sums(3)
    start_own(4)
    start_far(5)
    e3_copy().wait_recv()
    eigenvectors(e3, 1 - core)
    branch(0)
    branch(1)
    start_sums(4)
    start_own(5)
    start_far(6)
    branch(2)
    z_sum(0)
    branch(3)
    start_sums(5)
    start_own(6)
    start_far(7)
    z_sum(1)
    branch(4)
    z_sum(2)
    start_sums(6)
    start_own(7)
    z_sum(3)
    pl.semaphore_wait(near_z, 1)
    right_rotate(0)
    branch(5)
    start_sums(7)
    z_sum(4)
    branch(6)
    z_sum(5)
    right_rotate(1)
    branch(7)
    row_forward(0)
    z_sum(6)
    right_rotate(2)
    z_sum(7)
    right_rotate(3)
    row_forward(1)
    row_wait(0)
    row_forward(2)
    row_wait(1)
    left_rotate((0, 1, 2, 3), True)
    send_result(0)
    row_forward(3)
    row_wait(2)
    left_rotate((4, 5, 6), True)
    row_wait(3)
    left_rotate((7,), False)
    send_result(1)

    for d in range(1, NY):
        e1_copy(d).wait_send()
    for d in range(1, NZ):
        e2_copy(d).wait_send()
    e3_copy().wait_send()
    for u in range(UNITS):
        remote(part.at[0:3, 0], part.at[0:3, 0], y_s.at[u], yn_r.at[u], lat=right).wait_send()
    remote(spart.at[:, 0:NZ - 1], zin.at[:, 0:NZ - 1], z_s, z_r.at[0], lat=right).wait_send()
    for w in range(len(WINDOWS)):
        step1_all(w).wait_send()
        step2_all(w).wait_send()
    for k in (0, 1):
        for d in range(1, NY):
            o_in(k, d).wait_recv()
            o_copy(k, d).wait_send()


def per_device(n_row, g_wannier, lattice, degeneracy, qgrid, phonon_vectors, wannier_k, wannier_kq):
    n_r, modes, rows_m, wide = g_wannier.shape
    width = wide // 2
    points, nv, _ = phonon_vectors.shape
    full = -(-modes // 16) * 16
    vz = NY * nv

    g = jnp.transpose(g_wannier, (2, 0, 1, 3))
    tail = jnp.pad(g[:, :, full - 16:], ((0, 0), (0, 0), (0, full - modes), (0, 0)))

    phonon = jnp.transpose(phonon_vectors, (1, 0, 2))

    dma = pltpu.SemaphoreType.DMA
    vmem = pl.BlockSpec(memory_space=pltpu.VMEM)
    smem = pl.BlockSpec(memory_space=pltpu.SMEM)
    widths = [hi - lo for lo, hi in WINDOWS]
    out = pl.pallas_call(
        functools.partial(kernel, n_row),
        out_shape=jax.ShapeDtypeStruct((NY, 2, 4 * nv, wide), BF16),
        in_specs=[vmem, vmem, smem, smem, smem, vmem, vmem, vmem],
        out_specs=vmem,
        scratch_shapes=[
            pltpu.VMEM((points, rows_m, full, wide), BF16),
            pltpu.VMEM((UNITS, full, wide), BF16),
            pltpu.VMEM((UNITS, 2, full, wide), BF16),
            pltpu.VMEM((NY, nv, 2 * modes), BF16),
            pltpu.VMEM((NY, nv, 2 * modes), BF16),
            pltpu.VMEM((NZ, vz, 2 * modes), BF16),
            pltpu.VMEM((NZ, vz, 2 * modes), BF16),
            pltpu.VMEM((vz, 2 * modes), F32),
            pltpu.VMEM((2, NZ * vz, 2 * full), BF16),
            pltpu.VMEM((UNITS, NZ, vz, wide), BF16),
            pltpu.VMEM((UNITS, NZ, vz, wide), BF16),
            pltpu.VMEM((WINDOWS[-1][1], wide), F32),
            pltpu.VMEM((wide, wide), BF16),
            pltpu.VMEM((2, 2, width, width), F32),
            pltpu.VMEM((UNITS, 2 * n_row, wide), BF16),
            *[pltpu.VMEM((NH, n_row // NH, wide // n_row, w), BF16) for w in widths * 3],
            pltpu.VMEM((WINDOWS[-1][1] // 128, wide, 128), F32),
            pltpu.VMEM((2, 2, 4 * vz, width), F32),
            pltpu.VMEM((2, NY, 4 * nv, wide), BF16),
            dma((UNITS,)), dma((UNITS, 2)), dma((UNITS,)),
            dma((NY + NZ + 1,)), dma((NY + NZ + 1,)),
            dma, dma((UNITS,)), pltpu.SemaphoreType.REGULAR,
            *[dma((len(WINDOWS),))] * 4,
            dma((2, NY)), dma((2, NY)),
        ],
        compiler_params=pltpu.CompilerParams(
            collective_id=0, has_side_effects=True, vmem_limit_bytes=36 * 1024 * 1024),
        name="interpolate",
    )(g, tail, lattice.T, degeneracy, qgrid.T, phonon, wannier_k, wannier_kq)
    out = out.reshape(NY, 2, nv, 4, wide).transpose(2, 0, 1, 3, 4)
    return out.reshape(nv, points, 4, wide).astype(F32)


def solution(mesh):
    in_specs = (
        P("lat", None, "row", None),
        P("lat", None),
        P("lat"),
        P(),
        P(None, "lat", None),
        P(),
        P(),
    )
    out_specs = P("lat", None, "row", None)
    return jax.shard_map(
        functools.partial(per_device, mesh.shape["row"]),
        mesh=mesh, in_specs=in_specs, out_specs=out_specs, check_vma=False)
```

time: 100 us -> 90.9 us (0.909)
  Pallas kernels: 93.8 us -> 86.4 us
  other arithmetic: 1.57 us -> 0 us
    pallas_call x1, Pallas kernels: 93.8 us -> 86.4 us  [per_device(): pl.pallas_call(functools.partial(kernel, n_row), out_shape=jax.ShapeDtype...]
    unnamed x6 -> x13, local copies, waits for them, and re-layouts: 3.56 us -> 2.63 us
where the time goes in v3:
time: 90.9 us; the launch traced here: 90.3 us
  Pallas kernels  86.4 us (95%)
  local copies, waits for them, and re-layouts  3.77 us (4%)
    pallas_call x1, Pallas kernels, per_device(): pl.pallas_call(functools.partial(kernel, n_row), out_shape=jax.ShapeDtype...  86.4 us
    unnamed x13, local copies, waits for them, and re-layouts  2.63 us

profile of v3, /device:TPU:1, one launch (start us, length us, event | category | flops | bytes accessed | tf_op | source)
XLA Modules:
  0.0 90.3 jit_solution(15221641440873733701)
XLA Ops:
  0.0 0.0 copy-start
  0.0 0.0 copy-start.1
  0.0 0.0 copy-start.2
  0.0 0.0 copy-start.3
  0.0 0.0 copy-start.4
  0.0 0.0 copy-start.5
  0.0 2.6 %copy.11 = bf16[6,300,4,256]{3,1,0,2:T(8,128)(2,1)S(1)} copy(bf16[6,300,4,256]{3,2,1,0:T(4,128)(2,1)} %param.7) | data formatting | bytes 7372800 | tf_op args[0]
  2.7 0.0 copy-done
  2.7 0.0 copy-done.1
  2.7 0.0 copy-done.2
  2.7 0.0 copy-done.3
  2.7 0.0 copy-done.4
  2.8 0.0 copy-done.5
  2.8 86.4 %interpolate.1 = bf16[4,2,72,256]{3,2,1,0:T(8,128)(2,1)S(1)} custom-call(bf16[4,6,300,256]{3,2,1,0:T(8,128)(2,1)S(1)} %bitcast.11, bf16[4,6,16,256]{3,2,1,0:T(8,128)(2,1)S(1)} %pad.4.tail_ref, s32[3,6]{1,0:T(4,128)S(1)} %bitcast.13, s32[6]{0:T(128)S(1)} %copy-done.5, s32[3,8]{1,0:T(4,128)S(1)} %bitcast.14, bf16[18,8,600]{2,1,0:T(8,128)(2,1)S(1)} %bitcast.12, ...), custom_call_target="tpu_custom_call" | custom-call | tf_op jit(solution)/shard_map/interpolate/pallas_call | solution.py:427
  89.2 0.1 reshape.7
  89.4 1.0 %copy.9 = f32[18,4,2,4,256]{4,3,2,1,0:T(4,128)} copy(f32[18,4,2,4,256]{4,3,0,2,1:T(4,128)S(1)} %bitcast.15) | data formatting | bytes 1179648 | tf_op jit(solution)/shard_map/convert_element_type | solution.py:463
  (2 shorter events, 0.0 us)
Async XLA Ops:
  0.0 2.7 %copy-start = (bf16[8,128,256]{2,1,0:T(8,128)(2,1)S(1)}, bf16[8,128,256]{2,1,0:T(8,128)(2,1)}, u32[]{:S(2)}) copy-start(bf16[8,128,256]{2,1,0:T(8,128)(2,1)} %wkq_ref.1) | copy-start | bytes 1572868
  0.0 2.7 %copy-start.1 = (bf16[8,18,600]{2,0,1:T(8,128)(2,1)S(1)}, bf16[8,18,600]{2,0,1:T(8,128)(2,1)}, u32[]{:S(2)}) copy-start(bf16[8,18,600]{2,0,1:T(8,128)(2,1)} %param.11) | copy-start | bytes 518404
  0.0 2.7 %copy-start.2 = (bf16[128,256]{1,0:T(8,128)(2,1)S(1)}, bf16[128,256]{1,0:T(8,128)(2,1)}, u32[]{:S(2)}) copy-start(bf16[128,256]{1,0:T(8,128)(2,1)} %wk_ref.1) | copy-start | bytes 196612
  0.0 2.7 %copy-start.3 = (s32[6,3]{0,1:T(4,128)S(1)}, s32[6,3]{0,1:T(4,128)}, u32[]{:S(2)}) copy-start(s32[6,3]{0,1:T(4,128)} %param.8) | copy-start | bytes 220
  0.0 2.7 %copy-start.4 = (s32[8,3]{0,1:T(4,128)S(1)}, s32[8,3]{0,1:T(4,128)}, u32[]{:S(2)}) copy-start(s32[8,3]{0,1:T(4,128)} %param.10) | copy-start | bytes 292
  0.0 2.7 %copy-start.5 = (s32[6]{0:T(128)S(1)}, s32[6]{0:T(128)}, u32[]{:S(2)}) copy-start(s32[6]{0:T(128)} %degeneracy_ref.1) | copy-start | bytes 76

commit v4 on v3

--- a/solution.py
+++ b/solution.py
@@ -12,6 +12,7 @@
 NY = 4
 NZ = 4
 NH = 4
+NX = 4
 MESH = pl.DeviceIdType.MESH
 F32 = jnp.float32
 BF16 = jnp.bfloat16
@@ -40,9 +41,9 @@
 
 
 def kernel(rows, g_ref, tail_ref, lattice_ref, degeneracy_ref, q_ref, e_ref, wk_ref, wkq_ref, out_ref,
-           part, yfar, ynear, e0, e1, e2, e3, ef, eb, spart, zin, sfull, rt, lf, lb,
+           part, yfar, ynear, e0, e1, e2, e3, ef, eb, spart, zin, sfull, rt, lb,
            kt0, kt1, kt2, kt3, km0, km1, km2, km3, kr0, kr1, kr2, kr3, zf, ob, osend,
-           y_s, yf_r, yn_r, e_s, e_r, z_s, z_r, near_z, r1_s, r1_r, r2_s, r2_r, o_s, o_r):
+           y_s, yf_r, yn_r, e_s, e_r, z_s, z_r, near_z, near_c, r1_s, r1_r, r2_s, r2_r, o_s, o_r):
     n_row = rows
     kt, km, kr = (kt0, kt1, kt2, kt3), (km0, km1, km2, km3), (kr0, kr1, kr2, kr3)
     lat = lax.axis_index("lat")
@@ -50,8 +51,8 @@
     y = lax.rem(lat, NY)
     z = lax.div(lat, NY)
     core = lax.rem(row, 2)
-    n_xc = n_row // NH
-    zh, xc = lax.div(row, n_xc), lax.rem(row, n_xc)
+    zh, x = lax.div(row, 2 * NX), lax.rem(lax.div(row, 2), NX)
+    group, n_group = zh * 2 + core, 2 * NH
     n_r, modes = g_ref.shape[1], g_ref.shape[2]
     full = part.shape[2]
     nv = e_ref.shape[0]
@@ -64,10 +65,14 @@
         return lax.rem(z + d, NZ) * NY + y
 
     def zh_peer(d):
-        return lax.rem(row + n_xc * d, n_row)
-
-    def xc_peer(p):
-        return zh * n_xc + lax.rem(xc + p, n_xc)
+        return lax.rem(row + 2 * NX * d, n_row)
+
+    def x_peer(d):
+        return zh * 2 * NX + lax.rem(x + d, NX) * 2 + core
+
+    def group_peer(p):
+        to = lax.rem(group + p, n_group)
+        return lax.div(to, 2) * 2 * NX + x * 2 + lax.rem(to, 2)
 
     def remote(src, dst, ss, rs, **dev):
         return pltpu.make_async_remote_copy(
@@ -82,9 +87,9 @@
     for d in (1, NH - 1):
         pl.semaphore_signal(barrier, inc=1, device_id={"row": zh_peer(d)}, device_id_type=MESH)
 
-    @pl.loop(1, n_xc)
-    def _(p):
-        pl.semaphore_signal(barrier, inc=1, device_id={"row": xc_peer(p)}, device_id_type=MESH)
+    for d in range(1, NX):
+        pl.semaphore_signal(barrier, inc=1, device_id={"row": x_peer(d)}, device_id_type=MESH)
+    pl.semaphore_signal(barrier, inc=1, device_id={"row": row + 1 - 2 * core}, device_id_type=MESH)
 
     at_q, at_r = iota((16, 128), 0), iota((16, 128), 1)
     is_cos = at_r < n_r
@@ -218,36 +223,33 @@
             total = total + zin[u, lax.rem(z + d, NZ)].astype(F32)
         sfull[COLUMN[u]:COLUMN[u] + vz, :] = total
 
-    def step1(w, d):
-        to = lax.rem(zh + d, NH)
-        return remote(kt[w].at[to], km[w].at[zh], r1_s.at[w], r1_r.at[w], row=zh_peer(d))
+    def step1(w, p):
+        to = lax.rem(group + p, n_group)
+        return remote(kt[w].at[to], km[w].at[group], r1_s.at[w], r1_r.at[w], row=group_peer(p))
 
     def step1_all(w):
-        return remote(kt[w].at[0:NH - 1], km[w].at[0:NH - 1], r1_s.at[w], r1_r.at[w], row=zh_peer(1))
-
-    def step2(w, p):
-        return remote(km[w].at[:, lax.rem(xc + p, n_xc)], kr[w].at[:, xc], r2_s.at[w], r2_r.at[w], row=xc_peer(p))
+        return remote(kt[w].at[0:n_group - 1], km[w].at[0:n_group - 1], r1_s.at[w], r1_r.at[w], row=group_peer(1))
+
+    def step2(w, d):
+        return remote(km[w].at[:, lax.rem(x + d, NX)], kr[w].at[:, x], r2_s.at[w], r2_r.at[w], row=x_peer(d))
 
     def step2_all(w):
-        return remote(km[w].at[:, 0:n_xc - 1], kr[w].at[:, 0:n_xc - 1], r2_s.at[w], r2_r.at[w], row=xc_peer(1))
+        return remote(km[w].at[:, 0:NX - 1], kr[w].at[:, 0:NX - 1], r2_s.at[w], r2_r.at[w], row=x_peer(1))
 
     def right_rotate(w):
         lo, hi = WINDOWS[w]
         res = dot(rt[...], sfull[lo:hi, :].astype(BF16), ((1,), (1,)))
         kt[w][...] = res.reshape(kt[w].shape).astype(BF16)
-        for d in (2, 1, 3):
-            step1(w, d).start()
-        km[w][zh] = kt[w][zh]
+        for p in (4, 3, 5, 2, 6, 1, 7):
+            step1(w, p).start()
+        km[w][group] = kt[w][group]
 
     def row_forward(w):
         step1_all(w).wait_recv()
-
-        @pl.loop(1, n_xc)
-        def _(p):
-            step2(w, p).start()
-
-        for i in range(NH):
-            kr[w][i, xc] = km[w][i, xc]
+        for d in (2, 1, 3):
+            step2(w, d).start()
+        for i in range(n_group):
+            kr[w][i, x] = km[w][i, x]
 
     def row_wait(w):
         step2_all(w).wait_recv()
@@ -293,36 +295,38 @@
 
     def rotations():
         r, j = iota((256, 256), 0), iota((256, 256), 1)
-        perm = one_hot(j == ((r >> 2) & 1) * 128 + (r >> 3) * 4 + (r & 3))
+        block = (r >> 6) * 8 + ((r >> 3) & 3) * 2 + ((r >> 5) & 1)
+        perm = one_hot(j == ((r >> 2) & 1) * 128 + block * 4 + (r & 3))
         both = jnp.concatenate([wk_ref[...], times_i(wk_ref[...])], axis=0)
         rt[...] = dot(perm, both, ((1,), (1,))).astype(BF16)
-        for k in (0, 1):
-            for t in (0, 1):
-                lf[k, t] = wkq_ref[2 * y + k, :, 128 * t:128 * t + 128].astype(F32)
+        r, j = iota((n_row, 128), 0), iota((n_row, 128), 1)
+        block = (r >> 3) * 8 + (r & 3) * 2 + ((r >> 2) & 1)
         for u in range(UNITS):
             k, m = divmod(u, 4)
-            ur = lf[k, 0, pl.ds(m, n_row, stride=4), :]
-            ui = lf[k, 1, pl.ds(m, n_row, stride=4), :]
+            left_rows = dot(one_hot(j == block * 4 + m), wkq_ref[2 * y + k])
+            ur, ui = left_rows[:, :128], left_rows[:, 128:]
             lb[u] = jnp.concatenate([jnp.concatenate([ur, -ui], axis=1), jnp.concatenate([ui, ur], axis=1)],
                                     axis=0).astype(BF16)
         sfull[COLUMN[6] + vz:COLUMN[7], :] = jnp.zeros((COLUMN[7] - COLUMN[6] - vz, 256), F32)
         sfull[COLUMN[7] + vz:, :] = jnp.zeros((640 - COLUMN[7] - vz, 256), F32)
 
-    pl.semaphore_wait(barrier, NY + NZ - 2 + 2 + n_xc - 1)
-    pl.semaphore_signal(near_z, inc=1, device_id={"row": zh_peer(1)}, device_id_type=MESH)
     phase_sums(0)
+    pl.semaphore_wait(barrier, NY + NZ + NX)
     start_far(0)
     start_own(0)
+    pl.semaphore_signal(near_z, inc=1, device_id={"row": zh_peer(1)}, device_id_type=MESH)
     pick()
-    for d in range(1, NY):
+    for d in (2, 1, 3):
         e1_copy(d).start()
     e1[y] = e0[y]
     phase_sums(1)
     start_far(1)
+    phase_sums(2)
+    start_far(2)
     start_sums(0)
     start_own(1)
-    phase_sums(2)
-    start_far(2)
+    phase_sums(3)
+    start_far(3)
     for d in range(1, NY):
         e1_in(d).wait_recv()
     for yy in range(NY):
@@ -332,39 +336,39 @@
         e2_copy(d).start()
     start_sums(1)
     start_own(2)
-    phase_sums(3)
-    start_far(3)
+    start_far(4)
     rotations()
     start_sums(2)
     start_own(3)
-    start_far(4)
+    start_far(5)
+    pl.semaphore_wait(near_z, 1)
+    pl.semaphore_signal(near_c, inc=1, device_id={"row": row + 1 - 2 * core}, device_id_type=MESH)
     for d in range(1, NZ):
         e2_in(d).wait_recv()
     e3_copy().start()
     eigenvectors(e2, core)
     start_sums(3)
     start_own(4)
-    start_far(5)
+    start_far(6)
     e3_copy().wait_recv()
     eigenvectors(e3, 1 - core)
     branch(0)
     branch(1)
     start_sums(4)
     start_own(5)
-    start_far(6)
+    start_far(7)
     branch(2)
     z_sum(0)
     branch(3)
     start_sums(5)
     start_own(6)
-    start_far(7)
     z_sum(1)
     branch(4)
     z_sum(2)
     start_sums(6)
     start_own(7)
     z_sum(3)
-    pl.semaphore_wait(near_z, 1)
+    pl.semaphore_wait(near_c, 1)
     right_rotate(0)
     branch(5)
     start_sums(7)
@@ -382,9 +386,9 @@
     row_wait(0)
     row_forward(2)
     row_wait(1)
+    row_forward(3)
     left_rotate((0, 1, 2, 3), True)
     send_result(0)
-    row_forward(3)
     row_wait(2)
     left_rotate((4, 5, 6), True)
     row_wait(3)
@@ -443,15 +447,14 @@
             pltpu.VMEM((UNITS, NZ, vz, wide), BF16),
             pltpu.VMEM((WINDOWS[-1][1], wide), F32),
             pltpu.VMEM((wide, wide), BF16),
-            pltpu.VMEM((2, 2, width, width), F32),
             pltpu.VMEM((UNITS, 2 * n_row, wide), BF16),
-            *[pltpu.VMEM((NH, n_row // NH, wide // n_row, w), BF16) for w in widths * 3],
+            *[pltpu.VMEM((2 * NH, NX, wide // n_row, w), BF16) for w in widths * 3],
             pltpu.VMEM((WINDOWS[-1][1] // 128, wide, 128), F32),
             pltpu.VMEM((2, 2, 4 * vz, width), F32),
             pltpu.VMEM((2, NY, 4 * nv, wide), BF16),
             dma((UNITS,)), dma((UNITS, 2)), dma((UNITS,)),
             dma((NY + NZ + 1,)), dma((NY + NZ + 1,)),
-            dma, dma((UNITS,)), pltpu.SemaphoreType.REGULAR,
+            dma, dma((UNITS,)), pltpu.SemaphoreType.REGULAR, pltpu.SemaphoreType.REGULAR,
             *[dma((len(WINDOWS),))] * 4,
             dma((2, NY)), dma((2, NY)),
         ],

time: 90.9 us -> 88.7 us (0.976)
  Pallas kernels: 86.4 us -> 84.4 us
    pallas_call x1, Pallas kernels: 86.4 us -> 84.4 us  [per_device(): pl.pallas_call(functools.partial(kernel, n_row), out_shape=jax.ShapeDtype...]
where the time goes in v4:
time: 88.7 us; the launch traced here: 88.2 us
  Pallas kernels  84.4 us (95%)
  local copies, waits for them, and re-layouts  3.77 us (4%)
    pallas_call x1, Pallas kernels, per_device(): pl.pallas_call(functools.partial(kernel, n_row), out_shape=jax.ShapeDtype...  84.4 us
    unnamed x13, local copies, waits for them, and re-layouts  2.63 us

profile of v4, /device:TPU:1, one launch (start us, length us, event | category | flops | bytes accessed | tf_op | source)
XLA Modules:
  0.0 88.2 jit_solution(3678544717601803115)
XLA Ops:
  0.0 0.0 copy-start
  0.0 0.0 copy-start.1
  0.0 0.0 copy-start.2
  0.0 0.0 copy-start.3
  0.0 0.0 copy-start.4
  0.0 0.0 copy-start.5
  0.0 2.6 %copy.11 = bf16[6,300,4,256]{3,1,0,2:T(8,128)(2,1)S(1)} copy(bf16[6,300,4,256]{3,2,1,0:T(4,128)(2,1)} %param.7) | data formatting | bytes 7372800 | tf_op args[0]
  2.7 0.0 copy-done
  2.7 0.0 copy-done.1
  2.7 0.0 copy-done.2
  2.7 0.0 copy-done.3
  2.7 0.0 copy-done.4
  2.8 0.0 copy-done.5
  2.8 84.4 %interpolate.1 = bf16[4,2,72,256]{3,2,1,0:T(8,128)(2,1)S(1)} custom-call(bf16[4,6,300,256]{3,2,1,0:T(8,128)(2,1)S(1)} %bitcast.11, bf16[4,6,16,256]{3,2,1,0:T(8,128)(2,1)S(1)} %pad.4.tail_ref, s32[3,6]{1,0:T(4,128)S(1)} %bitcast.13, s32[6]{0:T(128)S(1)} %copy-done.5, s32[3,8]{1,0:T(4,128)S(1)} %bitcast.14, bf16[18,8,600]{2,1,0:T(8,128)(2,1)S(1)} %bitcast.12, ...), custom_call_target="tpu_custom_call" | custom-call | tf_op jit(solution)/shard_map/interpolate/pallas_call | solution.py:431
  87.1 0.1 reshape.7
  87.3 1.0 %copy.9 = f32[18,4,2,4,256]{4,3,2,1,0:T(4,128)} copy(f32[18,4,2,4,256]{4,3,0,2,1:T(4,128)S(1)} %bitcast.15) | data formatting | bytes 1179648 | tf_op jit(solution)/shard_map/convert_element_type | solution.py:466
  (2 shorter events, 0.0 us)
Async XLA Ops:
  0.0 2.7 %copy-start = (bf16[8,128,256]{2,1,0:T(8,128)(2,1)S(1)}, bf16[8,128,256]{2,1,0:T(8,128)(2,1)}, u32[]{:S(2)}) copy-start(bf16[8,128,256]{2,1,0:T(8,128)(2,1)} %wkq_ref.1) | copy-start | bytes 1572868
  0.0 2.7 %copy-start.1 = (bf16[8,18,600]{2,0,1:T(8,128)(2,1)S(1)}, bf16[8,18,600]{2,0,1:T(8,128)(2,1)}, u32[]{:S(2)}) copy-start(bf16[8,18,600]{2,0,1:T(8,128)(2,1)} %param.11) | copy-start | bytes 518404
  0.0 2.7 %copy-start.2 = (bf16[128,256]{1,0:T(8,128)(2,1)S(1)}, bf16[128,256]{1,0:T(8,128)(2,1)}, u32[]{:S(2)}) copy-start(bf16[128,256]{1,0:T(8,128)(2,1)} %wk_ref.1) | copy-start | bytes 196612
  0.0 2.7 %copy-start.3 = (s32[6,3]{0,1:T(4,128)S(1)}, s32[6,3]{0,1:T(4,128)}, u32[]{:S(2)}) copy-start(s32[6,3]{0,1:T(4,128)} %param.8) | copy-start | bytes 220
  0.0 2.7 %copy-start.4 = (s32[8,3]{0,1:T(4,128)S(1)}, s32[8,3]{0,1:T(4,128)}, u32[]{:S(2)}) copy-start(s32[8,3]{0,1:T(4,128)} %param.10) | copy-start | bytes 292
  0.0 2.7 %copy-start.5 = (s32[6]{0:T(128)S(1)}, s32[6]{0:T(128)}, u32[]{:S(2)}) copy-start(s32[6]{0:T(128)} %degeneracy_ref.1) | copy-start | bytes 76

commit v5 on v4

--- a/solution.py
+++ b/solution.py
@@ -38,14 +38,15 @@
 UNITS = 8
 COLUMN = (0, 72, 144, 216, 288, 360, 432, 512)
 WINDOWS = ((0, 256), (256, 384), (384, 512), (512, 640))
+LAST = len(WINDOWS) - 1
 
 
 def kernel(rows, g_ref, tail_ref, lattice_ref, degeneracy_ref, q_ref, e_ref, wk_ref, wkq_ref, out_ref,
            part, yfar, ynear, e0, e1, e2, e3, ef, eb, spart, zin, sfull, rt, lb,
-           kt0, kt1, kt2, kt3, km0, km1, km2, km3, kr0, kr1, kr2, kr3, zf, ob, osend,
-           y_s, yf_r, yn_r, e_s, e_r, z_s, z_r, near_z, near_c, r1_s, r1_r, r2_s, r2_r, o_s, o_r):
+           kt0, kt1, kt2, kt3, km0, km1, km2, kr0, kr1, kr2, kr3, zf, ob, osend,
+           y_s, yf_r, yn_r, e_s, e_r, z_s, z_r, near_z, near_c, near_x, r1_s, r1_r, r2_s, r2_r, o_s, o_r):
     n_row = rows
-    kt, km, kr = (kt0, kt1, kt2, kt3), (km0, km1, km2, km3), (kr0, kr1, kr2, kr3)
+    kt, km, kr = (kt0, kt1, kt2, kt3), (km0, km1, km2), (kr0, kr1, kr2, kr3)
     lat = lax.axis_index("lat")
     row = lax.axis_index("row")
     y = lax.rem(lat, NY)
@@ -79,15 +80,13 @@
             src_ref=src, dst_ref=dst, send_sem=ss, recv_sem=rs, device_id=dev, device_id_type=MESH)
 
     barrier = pltpu.get_barrier_semaphore()
-    for d in range(1, NY):
-        pl.semaphore_signal(barrier, inc=1, device_id={"lat": ypeer(d)}, device_id_type=MESH)
+    for d in (1, NH - 1):
+        pl.semaphore_signal(barrier, inc=1, device_id={"row": zh_peer(d)}, device_id_type=MESH)
     for d in range(1, NZ):
         pl.semaphore_signal(barrier, inc=1, device_id={"lat": zpeer(d)}, device_id_type=MESH)
-
-    for d in (1, NH - 1):
-        pl.semaphore_signal(barrier, inc=1, device_id={"row": zh_peer(d)}, device_id_type=MESH)
-
-    for d in range(1, NX):
+    for d in (2, 1, 3):
+        pl.semaphore_signal(barrier, inc=1, device_id={"lat": ypeer(d)}, device_id_type=MESH)
+    for d in (2, 1, 3):
         pl.semaphore_signal(barrier, inc=1, device_id={"row": x_peer(d)}, device_id_type=MESH)
     pl.semaphore_signal(barrier, inc=1, device_id={"row": row + 1 - 2 * core}, device_id_type=MESH)
 
@@ -240,9 +239,25 @@
         lo, hi = WINDOWS[w]
         res = dot(rt[...], sfull[lo:hi, :].astype(BF16), ((1,), (1,)))
         kt[w][...] = res.reshape(kt[w].shape).astype(BF16)
-        for p in (4, 3, 5, 2, 6, 1, 7):
-            step1(w, p).start()
-        km[w][group] = kt[w][group]
+        if w < LAST:
+            for p in (4, 3, 5, 2, 6, 1, 7):
+                step1(w, p).start()
+            km[w][group] = kt[w][group]
+
+    def straight(p):
+        to = lax.rem(row + p, n_row)
+        at = (lax.div(to, 2 * NX) * 2 + lax.rem(to, 2)) * NX + lax.rem(lax.div(to, 2), NX)
+        return remote(kt[LAST].at[at], kr[LAST].at[group * NX + x], r2_s.at[LAST], r2_r.at[LAST], row=to)
+
+    def straight_all():
+        return remote(kt[LAST].at[0:n_row - 1], kr[LAST].at[0:n_row - 1], r2_s.at[LAST], r2_r.at[LAST],
+                      row=x_peer(1))
+
+    def start_straight(lo, hi):
+        @pl.loop(lo, hi)
+        def _(p):
+            straight(p).start()
+
 
     def row_forward(w):
         step1_all(w).wait_recv()
@@ -252,7 +267,7 @@
             kr[w][i, x] = km[w][i, x]
 
     def row_wait(w):
-        step2_all(w).wait_recv()
+        (step2_all(w) if w < LAST else straight_all()).wait_recv()
         lo, hi = WINDOWS[w]
         got = kr[w][...].astype(F32).reshape(8 * n_row, hi - lo)
         for t in range((hi - lo) // 128):
@@ -369,6 +384,8 @@
     start_own(7)
     z_sum(3)
     pl.semaphore_wait(near_c, 1)
+    for d in (2, 1, 3):
+        pl.semaphore_signal(near_x, inc=1, device_id={"row": x_peer(d)}, device_id_type=MESH)
     right_rotate(0)
     branch(5)
     start_sums(7)
@@ -382,11 +399,14 @@
     right_rotate(2)
     z_sum(7)
     right_rotate(3)
+    pl.semaphore_wait(near_x, NX - 1)
+    start_straight(12, n_row)
     row_forward(1)
+    start_straight(1, 12)
+    kr[LAST][group * NX + x] = kt[LAST][group * NX + x]
     row_wait(0)
     row_forward(2)
     row_wait(1)
-    row_forward(3)
     left_rotate((0, 1, 2, 3), True)
     send_result(0)
     row_wait(2)
@@ -403,9 +423,10 @@
     for u in range(UNITS):
         remote(part.at[0:3, 0], part.at[0:3, 0], y_s.at[u], yn_r.at[u], lat=right).wait_send()
     remote(spart.at[:, 0:NZ - 1], zin.at[:, 0:NZ - 1], z_s, z_r.at[0], lat=right).wait_send()
-    for w in range(len(WINDOWS)):
+    for w in range(LAST):
         step1_all(w).wait_send()
         step2_all(w).wait_send()
+    straight_all().wait_send()
     for k in (0, 1):
         for d in range(1, NY):
             o_in(k, d).wait_recv()
@@ -448,13 +469,16 @@
             pltpu.VMEM((WINDOWS[-1][1], wide), F32),
             pltpu.VMEM((wide, wide), BF16),
             pltpu.VMEM((UNITS, 2 * n_row, wide), BF16),
-            *[pltpu.VMEM((2 * NH, NX, wide // n_row, w), BF16) for w in widths * 3],
+            *[pltpu.VMEM((2 * NH, NX, wide // n_row, w), BF16) for w in widths[:-1]],
+            pltpu.VMEM((n_row, wide // n_row, widths[-1]), BF16),
+            *[pltpu.VMEM((2 * NH, NX, wide // n_row, w), BF16) for w in widths[:-1] * 2],
+            pltpu.VMEM((n_row, wide // n_row, widths[-1]), BF16),
             pltpu.VMEM((WINDOWS[-1][1] // 128, wide, 128), F32),
             pltpu.VMEM((2, 2, 4 * vz, width), F32),
             pltpu.VMEM((2, NY, 4 * nv, wide), BF16),
             dma((UNITS,)), dma((UNITS, 2)), dma((UNITS,)),
             dma((NY + NZ + 1,)), dma((NY + NZ + 1,)),
-            dma, dma((UNITS,)), pltpu.SemaphoreType.REGULAR, pltpu.SemaphoreType.REGULAR,
+            dma, dma((UNITS,)), *[pltpu.SemaphoreType.REGULAR] * 3,
             *[dma((len(WINDOWS),))] * 4,
             dma((2, NY)), dma((2, NY)),
         ],

time: 88.7 us -> 88.2 us (level)
  Pallas kernels: 84.4 us -> 83.2 us
    pallas_call x1, Pallas kernels: 84.4 us -> 83.2 us  [per_device(): pl.pallas_call(functools.partial(kernel, n_row), out_shape=jax.ShapeDtype...]
where the time goes in v5:
time: 88.2 us; the launch traced here: 87.1 us
  Pallas kernels  83.2 us (94%)
  local copies, waits for them, and re-layouts  3.77 us (4%)
    pallas_call x1, Pallas kernels, per_device(): pl.pallas_call(functools.partial(kernel, n_row), out_shape=jax.ShapeDtype...  83.2 us
    unnamed x13, local copies, waits for them, and re-layouts  2.63 us

profile of v5, /device:TPU:1, one launch (start us, length us, event | category | flops | bytes accessed | tf_op | source)
XLA Modules:
  0.0 87.1 jit_solution(6070845280476553578)
XLA Ops:
  0.0 0.0 copy-start
  0.0 0.0 copy-start.1
  0.0 0.0 copy-start.2
  0.0 0.0 copy-start.3
  0.0 0.0 copy-start.4
  0.0 0.0 copy-start.5
  0.0 2.6 %copy.11 = bf16[6,300,4,256]{3,1,0,2:T(8,128)(2,1)S(1)} copy(bf16[6,300,4,256]{3,2,1,0:T(4,128)(2,1)} %param.7) | data formatting | bytes 7372800 | tf_op args[0]
  2.7 0.0 copy-done
  2.7 0.0 copy-done.1
  2.7 0.0 copy-done.2
  2.7 0.0 copy-done.3
  2.7 0.0 copy-done.4
  2.8 0.0 copy-done.5
  2.8 83.2 %interpolate.1 = bf16[4,2,72,256]{3,2,1,0:T(8,128)(2,1)S(1)} custom-call(bf16[4,6,300,256]{3,2,1,0:T(8,128)(2,1)S(1)} %bitcast.11, bf16[4,6,16,256]{3,2,1,0:T(8,128)(2,1)S(1)} %pad.4.tail_ref, s32[3,6]{1,0:T(4,128)S(1)} %bitcast.13, s32[6]{0:T(128)S(1)} %copy-done.5, s32[3,8]{1,0:T(4,128)S(1)} %bitcast.14, bf16[18,8,600]{2,1,0:T(8,128)(2,1)S(1)} %bitcast.12, ...), custom_call_target="tpu_custom_call" | custom-call | tf_op jit(solution)/shard_map/interpolate/pallas_call | solution.py:452
  86.0 0.1 reshape.7
  86.1 1.0 %copy.9 = f32[18,4,2,4,256]{4,3,2,1,0:T(4,128)} copy(f32[18,4,2,4,256]{4,3,0,2,1:T(4,128)S(1)} %bitcast.15) | data formatting | bytes 1179648 | tf_op jit(solution)/shard_map/convert_element_type | solution.py:490
  (2 shorter events, 0.0 us)
Async XLA Ops:
  0.0 2.7 %copy-start = (bf16[8,128,256]{2,1,0:T(8,128)(2,1)S(1)}, bf16[8,128,256]{2,1,0:T(8,128)(2,1)}, u32[]{:S(2)}) copy-start(bf16[8,128,256]{2,1,0:T(8,128)(2,1)} %wkq_ref.1) | copy-start | bytes 1572868
  0.0 2.7 %copy-start.1 = (bf16[8,18,600]{2,0,1:T(8,128)(2,1)S(1)}, bf16[8,18,600]{2,0,1:T(8,128)(2,1)}, u32[]{:S(2)}) copy-start(bf16[8,18,600]{2,0,1:T(8,128)(2,1)} %param.11) | copy-start | bytes 518404
  0.0 2.7 %copy-start.2 = (bf16[128,256]{1,0:T(8,128)(2,1)S(1)}, bf16[128,256]{1,0:T(8,128)(2,1)}, u32[]{:S(2)}) copy-start(bf16[128,256]{1,0:T(8,128)(2,1)} %wk_ref.1) | copy-start | bytes 196612
  0.0 2.7 %copy-start.3 = (s32[6,3]{0,1:T(4,128)S(1)}, s32[6,3]{0,1:T(4,128)}, u32[]{:S(2)}) copy-start(s32[6,3]{0,1:T(4,128)} %param.8) | copy-start | bytes 220
  0.0 2.7 %copy-start.4 = (s32[8,3]{0,1:T(4,128)S(1)}, s32[8,3]{0,1:T(4,128)}, u32[]{:S(2)}) copy-start(s32[8,3]{0,1:T(4,128)} %param.10) | copy-start | bytes 292
  0.0 2.7 %copy-start.5 = (s32[6]{0:T(128)S(1)}, s32[6]{0:T(128)}, u32[]{:S(2)}) copy-start(s32[6]{0:T(128)} %degeneracy_ref.1) | copy-start | bytes 76
